TPU v7x, 32 devices: a whole 2x2x4 slice. The times are simulated.
32 devices in a mesh: dp: 16 (over z, y, x), branch: 2 (over core).
Axes of the slice: x: 2, y: 2, z: 4, core: 2. Of those that a mesh axis runs over, the one named last changes fastest.
Arguments:
- node_states: bfloat16 [32768, 256], P(('dp', 'branch'))
- cotangent: bfloat16 [32768, 256], P(('dp', 'branch')), may hold values from -6 to 6
- counts: int32 [512], P('dp'), may hold values from 3 to 51, as said below
- bond_types: int32 [512, 64, 64], P('dp'), may hold values from 0 to 5, as said below
- edge_table: float32 [5, 256], replicated, may hold values from -3 to 3
- gine_weight_one: bfloat16 [256, 256], replicated, may hold values from -0.375 to 0.375
- gine_bias_one: float32 [256], replicated, may hold values from -2 to 2
- gine_weight_two: bfloat16 [256, 256], replicated, may hold values from -0.375 to 0.375
- gine_gain: float32 [256], replicated, may hold values from 0.5 to 1.5
- gine_shift: float32 [256], replicated, may hold values from -2 to 2
- query_weight: bfloat16 [256, 256], replicated, may hold values from -0.375 to 0.375
- query_bias: float32 [256], replicated, may hold values from -2 to 2
- key_weight: bfloat16 [256, 256], replicated, may hold values from -0.375 to 0.375
- value_weight: bfloat16 [256, 256], replicated, may hold values from -0.375 to 0.375
- out_weight: bfloat16 [256, 256], replicated, may hold values from -1 to 1
- attn_gain: float32 [256], replicated, may hold values from 0.5 to 1.5
- attn_shift: float32 [256], replicated, may hold values from -2 to 2
- ffn_weight_up: bfloat16 [256, 512], replicated, may hold values from -0.375 to 0.375
- ffn_bias_up: float32 [512], replicated, may hold values from -2 to 2
- ffn_weight_down: bfloat16 [512, 256], replicated, may hold values from -0.25 to 0.25
- final_gain: float32 [256], replicated, may hold values from 0.5 to 1.5
- final_shift: float32 [256], replicated, may hold values from -2 to 2
Outputs:
- layer_output: bfloat16 [32768, 256], P(('dp', 'branch'))
- node_grads: float32 [32768, 256], P(('dp', 'branch'))
- edge_table_grad: float32 [5, 256], replicated
- gine_weight_one_grad: float32 [256, 256], replicated
- gine_bias_one_grad: float32 [256], replicated
- gine_weight_two_grad: float32 [256, 256], replicated
- gine_gain_grad: float32 [256], replicated
- gine_shift_grad: float32 [256], replicated
- query_weight_grad: float32 [256, 256], replicated
- query_bias_grad: float32 [256], replicated
- key_weight_grad: float32 [256, 256], replicated
- value_weight_grad: float32 [256, 256], replicated
- out_weight_grad: float32 [256, 256], replicated
- attn_gain_grad: float32 [256], replicated
- attn_shift_grad: float32 [256], replicated
- ffn_weight_up_grad: float32 [256, 512], replicated
- ffn_bias_up_grad: float32 [512], replicated
- ffn_weight_down_grad: float32 [512, 256], replicated
- final_gain_grad: float32 [256], replicated
- final_shift_grad: float32 [256], replicated
Inputs may be any that keep to these rules, and one draw needn't show every extreme that they name: `counts`: nodes of each molecule; some molecule has exactly 51 nodes and some exactly 3. `bond_types`: symmetric, 0 on the diagonal and wherever a slot is not below its molecule's count; every molecule's consecutive nodes are bonded.
All inputs are finite; a program needn't handle non-finite values.
Results may differ from a plain program's by a relative error of at most 0.023.
Values may be sent and summed in bfloat16 or wider, within the bound.
A program may use at most 128 MiB of HBM per device.

v0:
```python
import math

import jax
import jax.numpy as jnp
from jax import lax
from jax.sharding import PartitionSpec as P

HEADS = 8
SLOT = 64


epsilon = 1e-05
masked_score = -1e30


def silu_slope(values):
    sigma = jax.nn.sigmoid(values)
    return sigma * (1.0 + values * (1.0 - sigma))


def graph_mask(sizes):
    return (jnp.arange(SLOT)[None, :] < sizes[:, None]).reshape(-1).astype(jnp.float32)


def blank_like(params):
    return tuple((jnp.zeros(item.shape, jnp.float32) for item in params))


def gine_forward(states, bonds, edge_table, weight_one, bias_one, weight_two):
    floats = states.astype(jnp.float32)
    kinds = edge_table.shape[0]
    graphs = bonds.shape[0]
    width = states.shape[1]
    shifted = floats[None] + edge_table[:, None, :]
    sent = jax.nn.silu(shifted).astype(jnp.bfloat16)
    onehot = (bonds[None] == (1 + jnp.arange(kinds))[:, None, None, None]).astype(jnp.bfloat16)
    message = jnp.einsum(
        "tgij,tgjd->gid",
        onehot,
        sent.reshape(kinds, graphs, SLOT, width),
        preferred_element_type=jnp.float32,
    ).reshape(-1, width)
    joined = (floats + message).astype(jnp.bfloat16)
    gine_first = jnp.dot(joined, weight_one, preferred_element_type=jnp.float32) + bias_one
    gine_act = jax.nn.silu(gine_first).astype(jnp.bfloat16)
    gine_last = jnp.dot(gine_act, weight_two, preferred_element_type=jnp.float32)
    return (gine_last + floats, (shifted, onehot, joined, gine_first, gine_act))


def gine_backward(grad_pre, states, bonds, edge_table, weight_one, bias_one, weight_two):
    unused, saved = gine_forward(states, bonds, edge_table, weight_one, bias_one, weight_two)
    shifted, onehot, joined, gine_first, gine_act = saved
    kinds = edge_table.shape[0]
    graphs = bonds.shape[0]
    width = states.shape[1]
    two_in = grad_pre.astype(jnp.bfloat16)
    weight_two_grad = jnp.einsum("rd,re->de", gine_act, two_in, preferred_element_type=jnp.float32)
    act_grad = jnp.einsum("re,de->rd", two_in, weight_two, preferred_element_type=jnp.float32)
    one_in = (act_grad * silu_slope(gine_first)).astype(jnp.bfloat16)
    weight_one_grad = jnp.einsum("rd,re->de", joined, one_in, preferred_element_type=jnp.float32)
    bias_one_grad = jnp.sum(one_in.astype(jnp.float32), axis=0)
    joined_back = jnp.einsum("re,de->rd", one_in, weight_one, preferred_element_type=jnp.float32)
    message_grad = joined_back.astype(jnp.bfloat16).reshape(graphs, SLOT, width)
    sent_grad = jnp.einsum(
        "tgij,gid->tgjd", onehot, message_grad, preferred_element_type=jnp.float32
    ).reshape(kinds, -1, width)
    shifted_grad = sent_grad * silu_slope(shifted)
    table_grad = jnp.sum(shifted_grad, axis=1)
    grad_states = grad_pre + joined_back + jnp.sum(shifted_grad, axis=0)
    return (grad_states, (table_grad, weight_one_grad, bias_one_grad, weight_two_grad))


def attend_forward(states, present, query_weight, query_bias, key_weight, value_weight, out_weight):
    rows, width = states.shape
    graphs = rows // SLOT
    head_size = width // HEADS
    scaling = 1.0 / math.sqrt(head_size)
    query = (
        (jnp.dot(states, query_weight, preferred_element_type=jnp.float32) + query_bias)
        .astype(jnp.bfloat16)
        .reshape(graphs, SLOT, HEADS, head_size)
    )
    keys = (
        jnp.dot(states, key_weight, preferred_element_type=jnp.float32)
        .astype(jnp.bfloat16)
        .reshape(graphs, SLOT, HEADS, head_size)
    )
    values = (
        jnp.dot(states, value_weight, preferred_element_type=jnp.float32)
        .astype(jnp.bfloat16)
        .reshape(graphs, SLOT, HEADS, head_size)
    )
    live_keys = present.reshape(graphs, 1, 1, SLOT) > 0.5
    scores = (
        jnp.einsum("gihe,gjhe->ghij", query, keys, preferred_element_type=jnp.float32) * scaling
    )
    probs = jax.nn.softmax(jnp.where(live_keys, scores, masked_score), axis=-1)
    weights = probs.astype(jnp.bfloat16)
    mixed = (
        jnp.einsum("ghij,gjhe->gihe", weights, values, preferred_element_type=jnp.float32)
        .reshape(rows, width)
        .astype(jnp.bfloat16)
    )
    attn_out = jnp.dot(mixed, out_weight, preferred_element_type=jnp.float32)
    return (attn_out + states.astype(jnp.float32), (query, keys, values, probs, weights, mixed))


def attend_backward(
    grad_pre, states, present, query_weight, query_bias, key_weight, value_weight, out_weight
):
    unused, saved = attend_forward(
        states, present, query_weight, query_bias, key_weight, value_weight, out_weight
    )
    query, keys, values, probs, weights, mixed = saved
    rows, width = states.shape
    graphs = rows // SLOT
    head_size = width // HEADS
    scaling = 1.0 / math.sqrt(head_size)
    out_in = grad_pre.astype(jnp.bfloat16)
    out_weight_grad = jnp.einsum("rd,re->de", mixed, out_in, preferred_element_type=jnp.float32)
    mixed_grad = (
        jnp.einsum("re,de->rd", out_in, out_weight, preferred_element_type=jnp.float32)
        .astype(jnp.bfloat16)
        .reshape(graphs, SLOT, HEADS, head_size)
    )
    probs_grad = jnp.einsum(
        "gihe,gjhe->ghij", mixed_grad, values, preferred_element_type=jnp.float32
    )
    values_grad = (
        jnp.einsum("ghij,gihe->gjhe", weights, mixed_grad, preferred_element_type=jnp.float32)
        .reshape(rows, width)
        .astype(jnp.bfloat16)
    )
    score_grad = (
        probs * (probs_grad - jnp.sum(probs * probs_grad, axis=-1, keepdims=True))
    ).astype(jnp.bfloat16)
    query_grad = (
        (
            jnp.einsum("ghij,gjhe->gihe", score_grad, keys, preferred_element_type=jnp.float32)
            * scaling
        )
        .reshape(rows, width)
        .astype(jnp.bfloat16)
    )
    key_grad = (
        (
            jnp.einsum("ghij,gihe->gjhe", score_grad, query, preferred_element_type=jnp.float32)
            * scaling
        )
        .reshape(rows, width)
        .astype(jnp.bfloat16)
    )
    query_weight_grad = jnp.einsum(
        "rd,re->de", states, query_grad, preferred_element_type=jnp.float32
    )
    query_bias_grad = jnp.sum(query_grad.astype(jnp.float32), axis=0)
    key_weight_grad = jnp.einsum("rd,re->de", states, key_grad, preferred_element_type=jnp.float32)
    value_weight_grad = jnp.einsum(
        "rd,re->de", states, values_grad, preferred_element_type=jnp.float32
    )
    grad_states = grad_pre + jnp.einsum(
        "re,de->rd", query_grad, query_weight, preferred_element_type=jnp.float32
    )
    grad_states = grad_states + jnp.einsum(
        "re,de->rd", key_grad, key_weight, preferred_element_type=jnp.float32
    )
    grad_states = grad_states + jnp.einsum(
        "re,de->rd", values_grad, value_weight, preferred_element_type=jnp.float32
    )
    return (
        grad_states,
        (query_weight_grad, query_bias_grad, key_weight_grad, value_weight_grad, out_weight_grad),
    )


def split_sides(vector, is_local):
    nothing = jnp.zeros_like(vector)
    return (jnp.where(is_local, vector, nothing), jnp.where(is_local, nothing, vector))


def body(
    node_states,
    cotangent,
    counts,
    bond_types,
    edge_table,
    gine_weight_one,
    gine_bias_one,
    gine_weight_two,
    gine_gain,
    gine_shift,
    query_weight,
    query_bias,
    key_weight,
    value_weight,
    out_weight,
    attn_gain,
    attn_shift,
    ffn_weight_up,
    ffn_bias_up,
    ffn_weight_down,
    final_gain,
    final_shift,
):
    branch_side = lax.axis_index("branch")
    on_first = branch_side == 0
    half_graphs = counts.shape[0] // 2
    own_counts = lax.dynamic_slice_in_dim(counts, branch_side * half_graphs, half_graphs)
    own_present = graph_mask(own_counts)[:, None]
    own_total = jnp.sum(own_present)
    gine_params = (edge_table, gine_weight_one, gine_bias_one, gine_weight_two)
    attn_params = (query_weight, query_bias, key_weight, value_weight, out_weight)
    group_states = lax.all_gather(node_states, "branch", axis=0, tiled=True)
    group_present = graph_mask(counts)[:, None]
    branch_pre = lax.cond(
        on_first,
        lambda: gine_forward(group_states, bond_types, *gine_params)[0],
        lambda: attend_forward(group_states, group_present[:, 0], *attn_params)[0],
    )
    entries = [(branch_pre, group_present, on_first)]
    values, present, is_local = entries[0]
    part_local, part_global = split_sides(jnp.sum(present * values, axis=0), is_local)
    sum_local = part_local
    sum_global = part_global
    total_local, total_global, node_total = lax.psum(
        (sum_local, sum_global, own_total), ("dp", "branch")
    )
    mean_local = total_local / node_total
    mean_global = total_global / node_total
    values, present, is_local = entries[0]
    offset = values - jnp.where(is_local, mean_local, mean_global)
    part_local, part_global = split_sides(jnp.sum(present * offset * offset, axis=0), is_local)
    square_local = part_local
    square_global = part_global
    square_local, square_global = lax.psum((square_local, square_global), ("dp", "branch"))
    var_local = square_local / node_total
    var_global = square_global / node_total
    rstd_local = lax.rsqrt(var_local + epsilon)
    rstd_global = lax.rsqrt(var_global + epsilon)
    values, present, is_local = entries[0]
    whitened = (values - jnp.where(is_local, mean_local, mean_global)) * jnp.where(
        is_local, rstd_local, rstd_global
    )
    whitened_list = [whitened]
    normed_list = present * (
        jnp.where(is_local, gine_gain, attn_gain) * whitened
        + jnp.where(is_local, gine_shift, attn_shift)
    )
    joined_h = lax.psum_scatter(
        normed_list.astype(jnp.bfloat16), "branch", scatter_dimension=0, tiled=True
    ).astype(jnp.float32)
    hidden_in = joined_h.astype(jnp.bfloat16)
    up_pre = jnp.dot(hidden_in, ffn_weight_up, preferred_element_type=jnp.float32) + ffn_bias_up
    up_act = jax.nn.silu(up_pre).astype(jnp.bfloat16)
    ffn_pre = joined_h + jnp.dot(up_act, ffn_weight_down, preferred_element_type=jnp.float32)
    final_total = lax.psum(jnp.sum(own_present * ffn_pre, axis=0), ("dp", "branch"))
    final_mean = final_total / node_total
    final_offset = ffn_pre - final_mean
    final_square = lax.psum(
        jnp.sum(own_present * final_offset * final_offset, axis=0), ("dp", "branch")
    )
    final_var = final_square / node_total
    final_rstd = lax.rsqrt(final_var + epsilon)
    final_hat = (ffn_pre - final_mean) * final_rstd
    layer_output = (own_present * (final_gain * final_hat + final_shift)).astype(jnp.bfloat16)
    out_grad = own_present * cotangent.astype(jnp.float32)
    final_shift_grad, final_gain_grad = lax.psum(
        (jnp.sum(out_grad, axis=0), jnp.sum(out_grad * final_hat, axis=0)), ("dp", "branch")
    )
    grad_y = (
        own_present
        * final_gain
        * final_rstd
        * (out_grad - final_shift_grad / node_total - final_hat * final_gain_grad / node_total)
    )
    down_in = grad_y.astype(jnp.bfloat16)
    ffn_weight_down_grad = jnp.einsum(
        "rf,rd->fd", up_act, down_in, preferred_element_type=jnp.float32
    )
    up_in = (
        jnp.einsum("rd,fd->rf", down_in, ffn_weight_down, preferred_element_type=jnp.float32)
        * silu_slope(up_pre)
    ).astype(jnp.bfloat16)
    ffn_weight_up_grad = jnp.einsum(
        "rd,rf->df", hidden_in, up_in, preferred_element_type=jnp.float32
    )
    ffn_bias_up_grad = jnp.sum(up_in.astype(jnp.float32), axis=0)
    joined_grad = (
        grad_y + jnp.einsum("rf,df->rd", up_in, ffn_weight_up, preferred_element_type=jnp.float32)
    ).astype(jnp.bfloat16)
    incoming = [lax.all_gather(joined_grad, "branch", axis=0, tiled=True).astype(jnp.float32)]
    position = 0
    values, present, is_local = entries[position]
    masked = present * incoming[position]
    masked_grads = [masked]
    part_local, part_global = split_sides(jnp.sum(masked, axis=0), is_local)
    shift_local = part_local
    shift_global = part_global
    part_local, part_global = split_sides(
        jnp.sum(masked * whitened_list[position], axis=0), is_local
    )
    gine_shift_grad, attn_shift_grad, gine_gain_grad, attn_gain_grad = lax.psum(
        (shift_local, shift_global, part_local, part_global), ("dp", "branch")
    )
    pre_grads = []
    position = 0
    values, present, is_local = entries[position]
    scale_now = jnp.where(is_local, gine_gain, attn_gain) * jnp.where(
        is_local, rstd_local, rstd_global
    )
    shift_now = jnp.where(is_local, gine_shift_grad, attn_shift_grad)
    gain_now = jnp.where(is_local, gine_gain_grad, attn_gain_grad)
    pre_grads.append(
        present
        * scale_now
        * (
            masked_grads[position]
            - shift_now / node_total
            - whitened_list[position] * gain_now / node_total
        )
    )

    def gine_side():
        grad_states, gine_grads = gine_backward(
            pre_grads[0], group_states, bond_types, *gine_params
        )
        return (grad_states, gine_grads, blank_like(attn_params))

    def attend_side():
        grad_states, attn_grads = attend_backward(
            pre_grads[0], group_states, group_present[:, 0], *attn_params
        )
        return (grad_states, blank_like(gine_params), attn_grads)

    group_grads, gine_grads, attn_grads = lax.cond(on_first, gine_side, attend_side)
    node_grads = lax.psum_scatter(
        group_grads.astype(jnp.bfloat16), "branch", scatter_dimension=0, tiled=True
    ).astype(jnp.float32)
    table_grad, weight_one_grad, bias_one_grad, weight_two_grad = gine_grads
    query_weight_grad, query_bias_grad, key_weight_grad, value_weight_grad, out_weight_grad = (
        attn_grads
    )
    summed = lax.psum(
        (
            table_grad,
            weight_one_grad,
            bias_one_grad,
            weight_two_grad,
            query_weight_grad,
            query_bias_grad,
            key_weight_grad,
            value_weight_grad,
            out_weight_grad,
            ffn_weight_up_grad,
            ffn_bias_up_grad,
            ffn_weight_down_grad,
        ),
        ("dp", "branch"),
    )
    return (
        layer_output,
        node_grads,
        summed[0],
        summed[1],
        summed[2],
        summed[3],
        gine_gain_grad,
        gine_shift_grad,
        summed[4],
        summed[5],
        summed[6],
        summed[7],
        summed[8],
        attn_gain_grad,
        attn_shift_grad,
        summed[9],
        summed[10],
        summed[11],
        final_gain_grad,
        final_shift_grad,
    )


def solution(mesh):
    placed = (
        P(("dp", "branch"), None),
        P(("dp", "branch"), None),
        P("dp"),
        P("dp", None, None),
        P(),
        P(),
        P(),
        P(),
        P(),
        P(),
        P(),
        P(),
        P(),
        P(),
        P(),
        P(),
        P(),
        P(),
        P(),
        P(),
        P(),
        P(),
    )
    return jax.shard_map(
        body,
        mesh=mesh,
        in_specs=placed,
        out_specs=(
            P(("dp", "branch"), None),
            P(("dp", "branch"), None),
            P(),
            P(),
            P(),
            P(),
            P(),
            P(),
            P(),
            P(),
            P(),
            P(),
            P(),
            P(),
            P(),
            P(),
            P(),
            P(),
            P(),
            P(),
        ),
        check_vma=False,
    )
```

profile of v0, /device:TPU:0, one launch (start us, length us, event | category | flops | bytes accessed | tf_op | source)
XLA Modules:
  0.0 636.3 jit_solution(15744090706865574788)
XLA Ops:
  7.3 0.7 all-gather.3.cloned.1.call-update
  8.0 0.7 dynamic_slice.3
  8.7 0.7 fusion.97
  9.5 0.7 fusion.99
  10.2 1.2 broadcast_select_fusion.5
  11.4 9.9 %all-gather.3.cloned.1.call-done = bf16[2048,256]{1,0:T(8,128)(2,1)} async-done(((bf16[1024,256]{1,0:T(8,128)(2,1)}), bf16[2048,256]{1,0:T(8,128)(2,1)}) %all-gather.3.cloned.1.call-update) | async-done | bytes 1048592 | tf_op jit(solution)/shard_map/all_gather | solution.py:213
  21.4 8.0 %conditional.2 = (f32[2048,256]{1,0:T(8,128)S(1)}, bf16[2048,256]{1,0:T(8,128)(2,1)}) conditional(s32[]{:T(128)} %convert_element_type.197, (bf16[2048,256]{1,0:T(8,128)(2,1)}, bf16[256,256]{1,0:T(8,128)(2,1)}, f32[2048]{0:T(1024)S(1)}, bf16[256,256]{1,0:T(8,128)(2,1)}, f32[256]{0:T(256)}, /*index=5*/bf16[256,256]{1,0:T(8,128)(2,1)}, ...), branch_computations={%region_0.3_spmd, %region_3.0_spmd} | conditional | flops 1218971648 | bytes 57824440 | solution.py:215
  21.6 1.6 convert.2
  23.2 3.5 fusion.19
  27.0 0.6 copy-done.36
  27.6 1.7 fusion.25
  29.4 1.7 multiply_reduce_fusion.2
  31.1 67.1 %all-reduce.4 = (f32[256]{0:T(256)S(1)}, f32[256]{0:T(256)S(1)}, f32[]{:T(128)}) all-reduce(f32[256]{0:T(256)S(1)} %get-tuple-element.234, f32[256]{0:T(256)S(1)} %get-tuple-element.233, f32[]{:T(128)} %fusion.99), channel_id=1, replica_groups=mesh['dp'=16,'branch'=2] {'dp','branch'}, use_global_device_ids=true, to_apply=%region_8.9 | all-reduce | flops 513 | bytes 4104 | tf_op jit(solution)/shard_map/psum | solution.py:225
  98.2 0.6 divide_select_fusion
  99.3 41.3 %all-reduce.3 = (f32[256]{0:T(256)S(1)}, f32[256]{0:T(256)S(1)}) all-reduce(f32[256]{0:T(256)S(1)} %get-tuple-element.232, f32[256]{0:T(256)S(1)} %get-tuple-element.231), channel_id=1, replica_groups=mesh['dp'=16,'branch'=2] {'dp','branch'}, use_global_device_ids=true, to_apply=%region_11.12 | all-reduce | flops 512 | bytes 4096 | tf_op jit(solution)/shard_map/psum | solution.py:235
  140.6 1.2 fusion.101
  141.8 1.5 multiply_convert_fusion.8
  143.5 8.3 %reduce-scatter.3.cloned.1.call-done = bf16[1024,256]{1,0:T(8,128)(2,1)} async-done(((bf16[2048,256]{1,0:T(8,128)(2,1)}), bf16[1024,256]{1,0:T(8,128)(2,1)}) %reduce-scatter.3.cloned.1.call-update) | async-done | bytes 524304 | tf_op jit(solution)/shard_map/reduce_scatter | solution.py:249
  151.8 3.1 multiply_convert_fusion.7
  155.0 1.4 multiply_reduce_fusion.4
  156.4 40.5 %psum.180 = f32[256]{0:T(256)S(1)} all-reduce(f32[256]{0:T(256)S(1)} %get-tuple-element.237), channel_id=1, replica_groups=mesh['dp'=16,'branch'=2] {'dp','branch'}, use_global_device_ids=true, to_apply=%region_14.15 | all-reduce | flops 256 | bytes 2048 | tf_op jit(solution)/shard_map/psum | solution.py:256
  196.9 0.6 broadcast_divide_fusion.3
  197.5 1.4 fusion.92
  199.0 40.1 %psum.181 = f32[256]{0:T(256)S(1)} all-reduce(f32[256]{0:T(256)S(1)} %fusion.92), channel_id=1, replica_groups=mesh['dp'=16,'branch'=2] {'dp','branch'}, use_global_device_ids=true, to_apply=%region_16.17 | all-reduce | flops 256 | bytes 2048 | tf_op jit(solution)/shard_map/psum | solution.py:259
  239.0 0.6 add_rsqrt_fusion
  239.7 2.6 fusion.93
  242.2 40.4 %all-reduce.2 = (f32[256]{0:T(256)S(1)}, f32[256]{0:T(256)S(1)}) all-reduce(f32[256]{0:T(256)S(1)} %get-tuple-element.187, f32[256]{0:T(256)S(1)} %get-tuple-element.186), channel_id=1, replica_groups=mesh['dp'=16,'branch'=2] {'dp','branch'}, use_global_device_ids=true, to_apply=%region_20.21 | all-reduce | flops 512 | bytes 4096 | tf_op jit(solution)/shard_map/psum | solution.py:267
  282.7 0.6 broadcast_divide_fusion.4
  283.4 4.8 convert_reduce_fusion.2
  288.2 1.0 copy-done.30
  289.2 2.0 fusion.91
  291.3 9.0 %all-gather.5.cloned.1.call-done = bf16[2048,256]{1,0:T(8,128)(2,1)} async-done(((bf16[1024,256]{1,0:T(8,128)(2,1)}), bf16[2048,256]{1,0:T(8,128)(2,1)}) %all-gather.5.cloned.1.call-update) | async-done | bytes 1048592 | tf_op jit(solution)/shard_map/all_gather | solution.py:291
  300.2 1.9 fusion.90
  302.1 40.6 %all-reduce.1 = (f32[256]{0:T(256)S(1)}, f32[256]{0:T(256)S(1)}, f32[256]{0:T(256)S(1)}, f32[256]{0:T(256)S(1)}) all-reduce(f32[256]{0:T(256)S(1)} %get-tuple-element.230, f32[256]{0:T(256)S(1)} %get-tuple-element.229, f32[256]{0:T(256)S(1)} %get-tuple-element.228, ...), channel_id=1, replica_groups=mesh['dp'=16,'branch'=2] {'dp','branch'}, use_global_device_ids=true, to_apply=%region_25.26 | all-reduce | flops 1024 | bytes 8192 | tf_op jit(solution)/shard_map/psum | solution.py:302
  342.7 0.6 select_divide_fusion
  343.4 4.1 subtract_multiply_fusion
  347.6 27.8 %conditional.3 = (bf16[2048,256]{1,0:T(8,128)(2,1)S(1)}, f32[5,256]{1,0:T(8,128)S(1)}, f32[256,256]{1,0:T(8,128)S(1)}, f32[256]{0:T(256)S(1)}, f32[256,256]{1,0:...) conditional(s32[]{:T(128)} %convert_element_type.197, ...), branch_computations={%region_27.32_spmd, %region_32.36_spmd} | conditional | flops 3383215872 | bytes 215575056 | solution.py:335
  356.1 1.6 copy.128
  358.4 3.3 fusion.71
  362.0 0.6 copy-done.37
  363.0 1.1 copy-done.6
  364.2 0.8 fusion.84
  365.1 1.0 convert_reduce_fusion.1
  367.1 6.3 fusion.100
  373.4 0.5 bitcast_add_fusion.2
  373.9 0.7 broadcast.131.clone.2
  374.7 0.7 broadcast.131.clone
  375.5 0.9 copy-done.16
  376.5 2.7 fusion.107
  379.3 2.2 fusion.94
  381.5 0.8 copy.129
  382.3 0.8 copy.130
  383.2 0.8 copy.131
  384.0 125.7 %all-reduce = (f32[5,256]{1,0:T(8,128)}, f32[256]{0:T(256)}, f32[256]{0:T(256)}, f32[512]{0:T(512)}) all-reduce(f32[5,256]{1,0:T(8,128)S(1)} %get-tuple-element.122, f32[256]{0:T(256)S(1)} %get-tuple-element.124, f32[256]{0:T(256)S(1)} %get-tuple-element.127, f32[512]{0:T(512)S(1)} %copy-done.53), channel_id=1, replica_groups=mesh['dp'=16,'branch'=2] {'dp','branch'}, use_global_device_ids=true, to_apply=%region_37.38 | all-reduce | flops 2304 | bytes 18432 | tf_op jit(solution)/shard_map/psum | solution.py:343
  509.7 2.1 convert_element_type.210
  511.8 107.7 %all-reduce.8.cloned.1.call-done = (f32[256,256]{1,0:T(8,128)}, f32[256,256]{1,0:T(8,128)}, f32[256,256]{1,0:T(8,128)}, f32[256,256]{1,0:T(8,128)}, f32[256,256]...) async-done(((f32[256,256]{1,0:T(8,128)}, f32[256,256]{1,0:T(8,128)}, f32[256,256]{1,0:T(8,128)}, f32[256,256]{1,0:T(8,128)}, ...) | async-done | bytes 2621456 | tf_op jit(solution)/shard_map/psum | solution.py:343
  619.6 1.8 copy.206
  621.4 1.7 copy.207
  623.1 1.7 copy.208
  624.8 1.7 copy.209
  626.4 0.7 copy.210
  627.1 0.7 copy.211
  627.8 0.8 copy.212
  628.6 0.8 copy.213
  (138 shorter events, 4.0 us)
Async XLA Ops:
  7.2 144.6 %copy-start = (bf16[256,512]{1,0:T(8,128)(2,1)S(1)}, bf16[256,512]{1,0:T(8,128)(2,1)}, u32[]{:S(2)}) copy-start(bf16[256,512]{1,0:T(8,128)(2,1)} %param.43) | copy-start | bytes 786436
  7.2 14.1 %all-gather.3.cloned.1.call-start = ((), (), s32[]{:S(2)}) async-start(), calls=%async_computation.2 | async-start | bytes 1572864 | tf_op jit(solution)/shard_map/all_gather | solution.py:213
  7.9 143.9 %reduce-scatter.3.cloned.1.call-start = ((), (), s32[]{:S(2)}) async-start(), calls=%async_computation.3 | async-start | bytes 1572864 | tf_op jit(solution)/shard_map/reduce_scatter | solution.py:249
  8.7 12.6 %copy-start.68 = (s32[16]{0:T(128)}, s32[16]{0:T(128)S(1)}, u32[]{:S(2)}) copy-start(s32[16]{0:T(128)S(1)} %dynamic_slice.3) | copy-start | bytes 196
  21.6 1.6 copy-start.29
  21.6 1.6 copy-start.71
  23.2 3.6 copy-start.3
  26.7 0.9 copy-start.36
  26.7 0.9 copy-start.57
  29.4 69.5 %copy-start.4 = (bf16[2048,256]{1,0:T(8,128)(2,1)S(1)}, bf16[2048,256]{1,0:T(8,128)(2,1)}, u32[]{:S(2)}) copy-start(bf16[2048,256]{1,0:T(8,128)(2,1)} %get-tuple-element.120) | copy-start | bytes 3145732
  31.1 109.5 %copy-start.66 = (f32[256]{0:T(256)S(1)}, f32[256]{0:T(256)}, u32[]{:S(2)}) copy-start(f32[256]{0:T(256)} %param.34) | copy-start | bytes 3076
  31.1 109.5 %copy-start.67 = (f32[256]{0:T(256)S(1)}, f32[256]{0:T(256)}, u32[]{:S(2)}) copy-start(f32[256]{0:T(256)} %param.41) | copy-start | bytes 3076
  31.1 110.7 %copy-start.52 = (f32[256]{0:T(256)S(1)}, f32[256]{0:T(256)}, u32[]{:S(2)}) copy-start(f32[256]{0:T(256)} %broadcast_select_fusion.5) | copy-start | bytes 3076
  141.8 158.5 %copy-start.46 = (f32[256]{0:T(256)}, f32[256]{0:T(256)S(1)}, u32[]{:S(2)}) copy-start(f32[256]{0:T(256)S(1)} %get-tuple-element.213) | copy-start | bytes 3076
  141.8 1.6 copy-start.69
  141.8 10.0 %copy-start.73 = (f32[512]{0:T(512)S(1)}, f32[512]{0:T(512)}, u32[]{:S(2)}) copy-start(f32[512]{0:T(512)} %param.44) | copy-start | bytes 6148
  143.3 156.9 %all-gather.5.cloned.1.call-start = ((), (), s32[]{:S(2)}) async-start(), calls=%async_computation.4 | async-start | bytes 1572864 | tf_op jit(solution)/shard_map/all_gather | solution.py:291
  151.8 3.1 copy-start.20
  151.8 3.1 copy-start.42
  154.9 1.4 copy-start.31
  154.9 84.7 %copy-start.54 = (f32[256]{0:T(256)S(1)}, f32[256]{0:T(256)}, u32[]{:S(2)}) copy-start(f32[256]{0:T(256)} %param.47) | copy-start | bytes 3076
  155.0 84.7 %copy-start.55 = (f32[256]{0:T(256)S(1)}, f32[256]{0:T(256)}, u32[]{:S(2)}) copy-start(f32[256]{0:T(256)} %param.46) | copy-start | bytes 3076
  197.5 90.7 %copy-start.47 = (f32[256]{0:T(256)}, f32[256]{0:T(256)S(1)}, u32[]{:S(2)}) copy-start(f32[256]{0:T(256)S(1)} %broadcast_divide_fusion.3) | copy-start | bytes 3076
  239.7 48.5 %copy-start.49 = (f32[256]{0:T(256)}, f32[256]{0:T(256)S(1)}, u32[]{:S(2)}) copy-start(f32[256]{0:T(256)S(1)} %add_rsqrt_fusion) | copy-start | bytes 3076
  282.7 5.5 copy-start.63
  282.7 5.5 copy-start.74
  283.3 4.8 copy-start.64
  283.3 5.8 copy-start.11
  283.4 5.8 copy-start.33
  288.2 1.0 copy-start.30
  291.2 218.5 %reduce-scatter.5.cloned.1.call-start = ((), (), s32[]{:S(2)}) async-start(), calls=%async_computation.5 | async-start | bytes 1572864 | tf_op jit(solution)/shard_map/reduce_scatter | solution.py:336
  342.7 0.7 copy-start.59
  342.7 0.7 copy-start.60
  342.7 0.7 copy-start.61
  342.7 0.7 copy-start.62
  343.4 4.2 copy-start.21
  343.4 4.2 copy-start.22
  343.4 4.1 copy-start.24
  357.7 0.7 copy-start.72
  361.7 0.9 copy-start.37
  361.7 0.9 copy-start.58
  362.6 1.6 copy-start.6
  364.2 0.9 copy-start.70
  375.4 1.0 copy-start.16
  375.4 6.1 copy-start.27
  375.4 6.1 copy-start.28
  375.4 3.8 copy-start.12
  375.5 3.8 copy-start.48
  375.5 3.8 copy-start.50
  375.5 3.8 copy-start.56
  375.5 3.8 copy-start.65
  375.5 3.8 copy-start.75
  376.4 2.9 copy-start.32
  376.4 243.1 %all-reduce.8.cloned.1.call-start = ((), (), s32[]{:S(2)}) async-start(), calls=%async_computation.6 | async-start | bytes 5242880 | tf_op jit(solution)/shard_map/psum | solution.py:343
  376.5 2.8 copy-start.34
  379.3 3.9 copy-start.26
  381.5 2.5 copy-start.53
  619.6 6.8 %copy-start.41 = (f32[256,256]{1,0:T(8,128)S(1)}, f32[256,256]{1,0:T(8,128)}, u32[]{:S(2)}) copy-start(f32[256,256]{1,0:T(8,128)} %get-tuple-element.278) | copy-start | bytes 786436
  619.6 7.6 %copy-start.40 = (f32[256,256]{1,0:T(8,128)S(1)}, f32[256,256]{1,0:T(8,128)}, u32[]{:S(2)}) copy-start(f32[256,256]{1,0:T(8,128)} %get-tuple-element.279) | copy-start | bytes 786436
  619.6 8.3 %copy-start.39 = (f32[256,512]{1,0:T(8,128)S(1)}, f32[256,512]{1,0:T(8,128)}, u32[]{:S(2)}) copy-start(f32[256,512]{1,0:T(8,128)} %get-tuple-element.282) | copy-start | bytes 1572868
  619.6 9.1 %copy-start.38 = (f32[512,256]{1,0:T(8,128)S(1)}, f32[512,256]{1,0:T(8,128)}, u32[]{:S(2)}) copy-start(f32[512,256]{1,0:T(8,128)} %get-tuple-element.284) | copy-start | bytes 1572868
  621.4 8.1 %copy-start.1 = (bf16[256,512]{1,0:T(8,128)(2,1)S(1)}, bf16[256,512]{1,0:T(8,128)(2,1)}, u32[]{:S(2)}) copy-start(bf16[256,512]{1,0:T(8,128)(2,1)} %param.43) | copy-start | bytes 786436
Sparse Core Ops, SparseCore 0:
  9.6 11.7 all-gather.2
  143.4 8.3 reduce-scatter.2
  291.4 8.8 all-gather.4
  376.5 94.5 reduce-scatter.4
  479.1 140.4 all-reduce.7
where the time goes:
time: 648 us; the launch traced here: 636 us
  blocking collectives  396 us (61%)
  waiting for transfers between devices  136 us (21%)
  matrix products  34.4 us (5%)
  other arithmetic  25.6 us (4%)
  local copies, waits for them, and re-layouts  21.3 us (3%)
  between operations  14.7 us (2%)
  loops' own time  8.92 us (1%)
    psum x1, blocking collectives, body(): lax.psum((table_grad, weight_one_grad, bias_one_grad, weight_two_grad, qu...  126 us
    psum x1, waiting for transfers between devices, body(): lax.psum((table_grad, weight_one_grad, bias_one_grad, weight_two_grad, qu...  108 us
    psum x1, blocking collectives, body(): lax.psum((sum_local, sum_global, own_total), ('dp', 'branch'))  67.1 us
    psum x1, blocking collectives, body(): lax.psum((square_local, square_global), ('dp', 'branch'))  41.3 us
    psum x1, blocking collectives, body(): lax.psum((shift_local, shift_global, part_local, part_global), ('dp', 'br...  40.6 us
    psum x1, blocking collectives, body(): lax.psum(jnp.sum(own_present * ffn_pre, axis=0), ('dp', 'branch'))  40.5 us
    psum x1, blocking collectives, body(): lax.psum((jnp.sum(out_grad, axis=0), jnp.sum(out_grad * final_hat, axis=0...  40.4 us
    psum x1, blocking collectives, body(): lax.psum(jnp.sum(own_present * final_offset * final_offset, axis=0), ('dp...  40.1 us
  transfers between devices with their start and end apart: 5, of which 4 were waited for; matrix products, arithmetic and copies ran while one was open for 2% of the time, Pallas kernels for 0%

commit v1 on v0

--- a/solution.py
+++ b/solution.py
@@ -173,9 +173,11 @@
     )
 
 
-def split_sides(vector, is_local):
-    nothing = jnp.zeros_like(vector)
-    return (jnp.where(is_local, vector, nothing), jnp.where(is_local, nothing, vector))
+def norm_stats(values, present):
+    count = jnp.sum(present)
+    mean = jnp.sum(present * values, axis=0) / count
+    offset = values - mean
+    return (mean, jnp.sum(present * offset * offset, axis=0))
 
 
 def body(
@@ -202,180 +204,100 @@
     final_gain,
     final_shift,
 ):
-    branch_side = lax.axis_index("branch")
-    on_first = branch_side == 0
-    half_graphs = counts.shape[0] // 2
-    own_counts = lax.dynamic_slice_in_dim(counts, branch_side * half_graphs, half_graphs)
-    own_present = graph_mask(own_counts)[:, None]
-    own_total = jnp.sum(own_present)
+    axes = ("dp", "branch")
+    side = lax.axis_index("branch")
+    half = counts.shape[0] // 2
+    own_counts = lax.dynamic_slice_in_dim(counts, side * half, half)
+    own_bonds = lax.dynamic_slice_in_dim(bond_types, side * half, half)
+    present = graph_mask(own_counts)[:, None]
+    own_total = jnp.sum(present)
     gine_params = (edge_table, gine_weight_one, gine_bias_one, gine_weight_two)
     attn_params = (query_weight, query_bias, key_weight, value_weight, out_weight)
-    group_states = lax.all_gather(node_states, "branch", axis=0, tiled=True)
-    group_present = graph_mask(counts)[:, None]
-    branch_pre = lax.cond(
-        on_first,
-        lambda: gine_forward(group_states, bond_types, *gine_params)[0],
-        lambda: attend_forward(group_states, group_present[:, 0], *attn_params)[0],
-    )
-    entries = [(branch_pre, group_present, on_first)]
-    values, present, is_local = entries[0]
-    part_local, part_global = split_sides(jnp.sum(present * values, axis=0), is_local)
-    sum_local = part_local
-    sum_global = part_global
-    total_local, total_global, node_total = lax.psum(
-        (sum_local, sum_global, own_total), ("dp", "branch")
-    )
-    mean_local = total_local / node_total
-    mean_global = total_global / node_total
-    values, present, is_local = entries[0]
-    offset = values - jnp.where(is_local, mean_local, mean_global)
-    part_local, part_global = split_sides(jnp.sum(present * offset * offset, axis=0), is_local)
-    square_local = part_local
-    square_global = part_global
-    square_local, square_global = lax.psum((square_local, square_global), ("dp", "branch"))
-    var_local = square_local / node_total
-    var_global = square_global / node_total
-    rstd_local = lax.rsqrt(var_local + epsilon)
-    rstd_global = lax.rsqrt(var_global + epsilon)
-    values, present, is_local = entries[0]
-    whitened = (values - jnp.where(is_local, mean_local, mean_global)) * jnp.where(
-        is_local, rstd_local, rstd_global
-    )
-    whitened_list = [whitened]
-    normed_list = present * (
-        jnp.where(is_local, gine_gain, attn_gain) * whitened
-        + jnp.where(is_local, gine_shift, attn_shift)
-    )
-    joined_h = lax.psum_scatter(
-        normed_list.astype(jnp.bfloat16), "branch", scatter_dimension=0, tiled=True
-    ).astype(jnp.float32)
+    gine_pre, _ = gine_forward(node_states, own_bonds, *gine_params)
+    attn_pre, _ = attend_forward(node_states, present[:, 0], *attn_params)
+
+    def merge(stats):
+        means, squares, totals = lax.all_gather(stats, axes, axis=0)
+        node_total = jnp.sum(totals)
+        mean = jnp.sum(means * totals[:, None], axis=0) / node_total
+        shift = means - mean
+        square = jnp.sum(squares + totals[:, None] * shift * shift, axis=0)
+        return mean, lax.rsqrt(square / node_total + epsilon), node_total
+
+    both = jnp.concatenate([gine_pre, attn_pre], axis=1)
+    mean, squares = norm_stats(both, present)
+    mean, rstd, node_total = merge((mean, squares, own_total))
+    gains = jnp.concatenate([gine_gain, attn_gain])
+    shifts = jnp.concatenate([gine_shift, attn_shift])
+    width = node_states.shape[1]
+    hat = (both - mean) * rstd
+    normed = present * (gains * hat + shifts)
+    joined_h = normed[:, :width] + normed[:, width:]
     hidden_in = joined_h.astype(jnp.bfloat16)
     up_pre = jnp.dot(hidden_in, ffn_weight_up, preferred_element_type=jnp.float32) + ffn_bias_up
     up_act = jax.nn.silu(up_pre).astype(jnp.bfloat16)
     ffn_pre = joined_h + jnp.dot(up_act, ffn_weight_down, preferred_element_type=jnp.float32)
-    final_total = lax.psum(jnp.sum(own_present * ffn_pre, axis=0), ("dp", "branch"))
-    final_mean = final_total / node_total
-    final_offset = ffn_pre - final_mean
-    final_square = lax.psum(
-        jnp.sum(own_present * final_offset * final_offset, axis=0), ("dp", "branch")
-    )
-    final_var = final_square / node_total
-    final_rstd = lax.rsqrt(final_var + epsilon)
+    final_mean, final_squares = norm_stats(ffn_pre, present)
+    final_mean, final_rstd, _ = merge((final_mean, final_squares, own_total))
     final_hat = (ffn_pre - final_mean) * final_rstd
-    layer_output = (own_present * (final_gain * final_hat + final_shift)).astype(jnp.bfloat16)
-    out_grad = own_present * cotangent.astype(jnp.float32)
+    layer_output = (present * (final_gain * final_hat + final_shift)).astype(jnp.bfloat16)
+    out_grad = present * cotangent.astype(jnp.float32)
     final_shift_grad, final_gain_grad = lax.psum(
-        (jnp.sum(out_grad, axis=0), jnp.sum(out_grad * final_hat, axis=0)), ("dp", "branch")
+        (jnp.sum(out_grad, axis=0), jnp.sum(out_grad * final_hat, axis=0)), axes
     )
     grad_y = (
-        own_present
+        present
         * final_gain
         * final_rstd
         * (out_grad - final_shift_grad / node_total - final_hat * final_gain_grad / node_total)
     )
     down_in = grad_y.astype(jnp.bfloat16)
-    ffn_weight_down_grad = jnp.einsum(
-        "rf,rd->fd", up_act, down_in, preferred_element_type=jnp.float32
-    )
+    down_grad = jnp.einsum("rf,rd->fd", up_act, down_in, preferred_element_type=jnp.float32)
     up_in = (
         jnp.einsum("rd,fd->rf", down_in, ffn_weight_down, preferred_element_type=jnp.float32)
         * silu_slope(up_pre)
     ).astype(jnp.bfloat16)
-    ffn_weight_up_grad = jnp.einsum(
-        "rd,rf->df", hidden_in, up_in, preferred_element_type=jnp.float32
-    )
-    ffn_bias_up_grad = jnp.sum(up_in.astype(jnp.float32), axis=0)
-    joined_grad = (
+    up_grad = jnp.einsum("rd,rf->df", hidden_in, up_in, preferred_element_type=jnp.float32)
+    up_bias_grad = jnp.sum(up_in.astype(jnp.float32), axis=0)
+    joined_grad = present * (
         grad_y + jnp.einsum("rf,df->rd", up_in, ffn_weight_up, preferred_element_type=jnp.float32)
-    ).astype(jnp.bfloat16)
-    incoming = [lax.all_gather(joined_grad, "branch", axis=0, tiled=True).astype(jnp.float32)]
-    position = 0
-    values, present, is_local = entries[position]
-    masked = present * incoming[position]
-    masked_grads = [masked]
-    part_local, part_global = split_sides(jnp.sum(masked, axis=0), is_local)
-    shift_local = part_local
-    shift_global = part_global
-    part_local, part_global = split_sides(
-        jnp.sum(masked * whitened_list[position], axis=0), is_local
-    )
-    gine_shift_grad, attn_shift_grad, gine_gain_grad, attn_gain_grad = lax.psum(
-        (shift_local, shift_global, part_local, part_global), ("dp", "branch")
-    )
-    pre_grads = []
-    position = 0
-    values, present, is_local = entries[position]
-    scale_now = jnp.where(is_local, gine_gain, attn_gain) * jnp.where(
-        is_local, rstd_local, rstd_global
-    )
-    shift_now = jnp.where(is_local, gine_shift_grad, attn_shift_grad)
-    gain_now = jnp.where(is_local, gine_gain_grad, attn_gain_grad)
-    pre_grads.append(
-        present
-        * scale_now
-        * (
-            masked_grads[position]
-            - shift_now / node_total
-            - whitened_list[position] * gain_now / node_total
-        )
-    )
-
-    def gine_side():
-        grad_states, gine_grads = gine_backward(
-            pre_grads[0], group_states, bond_types, *gine_params
-        )
-        return (grad_states, gine_grads, blank_like(attn_params))
-
-    def attend_side():
-        grad_states, attn_grads = attend_backward(
-            pre_grads[0], group_states, group_present[:, 0], *attn_params
-        )
-        return (grad_states, blank_like(gine_params), attn_grads)
-
-    group_grads, gine_grads, attn_grads = lax.cond(on_first, gine_side, attend_side)
-    node_grads = lax.psum_scatter(
-        group_grads.astype(jnp.bfloat16), "branch", scatter_dimension=0, tiled=True
-    ).astype(jnp.float32)
-    table_grad, weight_one_grad, bias_one_grad, weight_two_grad = gine_grads
-    query_weight_grad, query_bias_grad, key_weight_grad, value_weight_grad, out_weight_grad = (
-        attn_grads
-    )
-    summed = lax.psum(
-        (
-            table_grad,
-            weight_one_grad,
-            bias_one_grad,
-            weight_two_grad,
-            query_weight_grad,
-            query_bias_grad,
-            key_weight_grad,
-            value_weight_grad,
-            out_weight_grad,
-            ffn_weight_up_grad,
-            ffn_bias_up_grad,
-            ffn_weight_down_grad,
-        ),
-        ("dp", "branch"),
+    ).astype(jnp.bfloat16).astype(jnp.float32)
+    twice = jnp.concatenate([joined_grad, joined_grad], axis=1)
+    shift_grads, gain_grads = lax.psum(
+        (jnp.sum(twice, axis=0), jnp.sum(twice * hat, axis=0)), axes
+    )
+    pre_grads = present * gains * rstd * (
+        twice - shift_grads / node_total - hat * gain_grads / node_total
+    )
+    gine_states, gine_grads = gine_backward(
+        pre_grads[:, :width], node_states, own_bonds, *gine_params
+    )
+    attn_states, attn_grads = attend_backward(
+        pre_grads[:, width:], node_states, present[:, 0], *attn_params
+    )
+    node_grads = gine_states + attn_states
+    table, one, bias_one, two, query, query_b, key, value, out, up, up_b, down = lax.psum(
+        (*gine_grads, *attn_grads, up_grad, up_bias_grad, down_grad), axes
     )
     return (
         layer_output,
         node_grads,
-        summed[0],
-        summed[1],
-        summed[2],
-        summed[3],
-        gine_gain_grad,
-        gine_shift_grad,
-        summed[4],
-        summed[5],
-        summed[6],
-        summed[7],
-        summed[8],
-        attn_gain_grad,
-        attn_shift_grad,
-        summed[9],
-        summed[10],
-        summed[11],
+        table,
+        one,
+        bias_one,
+        two,
+        gain_grads[:width],
+        shift_grads[:width],
+        query,
+        query_b,
+        key,
+        value,
+        out,
+        gain_grads[width:],
+        shift_grads[width:],
+        up,
+        up_b,
+        down,
         final_gain_grad,
         final_shift_grad,
     )

time: 648 us -> 528 us (0.81)
  blocking collectives: 396 us -> 313 us
  waiting for transfers between devices: 136 us -> 80.2 us
  local copies, waits for them, and re-layouts: 21.3 us -> 48 us
  loops' own time: 8.92 us -> 0 us
    psum x6 -> x2, blocking collectives: 355 us -> 81.4 us  [the longest x1 42.9 us: body(): lax.psum((jnp.sum(twice, axis=0), jnp.sum(twice * hat, axis=0)), axes)]
    all_gather x0 -> x4, blocking collectives: none -> 152 us  [merge(): means, squares, totals = lax.all_gather(stats, axes, axis=0)]
    unnamed x0 -> x1, blocking collectives: none -> 42 us
    psum x1, waiting for transfers between devices: 108 us -> 80.2 us  [body(): lax.psum((*gine_grads, *attn_grads, up_grad, up_bias_grad, down_grad), axes)]
    dot_general x0 -> x18, matrix products: none -> 19.2 us  [the longest x1 3.85 us: attend_backward(): jnp.einsum('ghij,gihe->gjhe', weights, mixed_grad, preferred_element_type...]
    all_gather x2 -> x0, waiting for transfers between devices: 18.9 us -> none  [the longest x1 9.9 us: body(): group_states = lax.all_gather(node_states, 'branch', axis=0, tiled=True)]
    unnamed x102 -> x172, local copies, waits for them, and re-layouts: 11.9 us -> 23.3 us
    convert_element_type x0 -> x13, local copies, waits for them, and re-layouts: none -> 9.06 us  [the longest x2 3.06 us: attend_backward(): key_grad = (jnp.einsum('ghij,gihe->gjhe', score_grad, query, preferred_el...]
  transfers between devices with their start and end apart: 5 -> 1, of which waited for: 4 -> 1; matrix products, arithmetic and copies ran while one was open for 2% -> 4% of each run, Pallas kernels for 0% -> 0%
where the time goes in v1:
time: 528 us; the launch traced here: 519 us
  blocking collectives  313 us (59%)
  waiting for transfers between devices  80.2 us (15%)
  local copies, waits for them, and re-layouts  48 us (9%)
  matrix products  40.5 us (8%)
  other arithmetic  21.8 us (4%)
  between operations  15.4 us (3%)
    all_gather x4, blocking collectives, merge(): means, squares, totals = lax.all_gather(stats, axes, axis=0)  152 us
    psum x1, waiting for transfers between devices, body(): lax.psum((*gine_grads, *attn_grads, up_grad, up_bias_grad, down_grad), axes)  80.2 us
    psum x1, blocking collectives, body(): lax.psum((jnp.sum(twice, axis=0), jnp.sum(twice * hat, axis=0)), axes)  42.9 us
    unnamed x1, blocking collectives  42 us
    psum x1, blocking collectives, body(): lax.psum((*gine_grads, *attn_grads, up_grad, up_bias_grad, down_grad), axes)  38.5 us
    psum x1, blocking collectives, body(): lax.psum((jnp.sum(out_grad, axis=0), jnp.sum(out_grad * final_hat, axis=0...  37.2 us
    unnamed x172, local copies, waits for them, and re-layouts  23.3 us
  transfers between devices with their start and end apart: 1, of which 1 were waited for; matrix products, arithmetic and copies ran while one was open for 4% of the time, Pallas kernels for 0%

profile of v1, /device:TPU:0, one launch (start us, length us, event | category | flops | bytes accessed | tf_op | source)
XLA Modules:
  0.0 518.5 jit_solution(3221021089230056894)
XLA Ops:
  7.3 0.9 dynamic_slice.6
  8.9 0.8 dynamic-update-slice
  9.7 42.0 %all-reduce = f32[32]{0:T(128)S(1)} all-reduce(f32[32]{0:T(128)S(1)} %dynamic-update-slice), channel_id=1, replica_groups=mesh['dp'=16,'branch'=2] {'dp','branch'}, use_global_device_ids=true, to_apply=%add | all-reduce | flops 32 | bytes 256
  52.4 1.1 copy.108
  53.7 1.0 copy.121
  55.2 1.7 reshape.176
  58.6 1.6 reshape.175
  60.5 4.1 fusion.10
  64.7 1.6 copy.111
  66.2 2.5 fusion.51
  68.7 3.0 fusion.77
  71.8 0.7 fusion.28
  72.5 1.2 copy-done.23
  73.8 0.7 copy.119
  74.5 1.5 convert_element_type.159
  80.0 40.3 %all-gather.5 = f32[32,1,512]{2,1,0:T(1,128)S(1)} all-gather(f32[1,1,512]{2,1,0:T(1,128)S(1)} %bitcast.120), channel_id=3, replica_groups=mesh['dp'=16,'branch'=2] {'dp','branch'}, dimensions={0}, use_global_device_ids=true | all-gather | bytes 67584 | tf_op jit(solution)/shard_map/all_gather | solution.py:220
  120.4 37.0 %all-gather.4 = f32[32,1,512]{2,1,0:T(1,128)S(1)} all-gather(f32[1,1,512]{2,1,0:T(1,128)S(1)} %bitcast.118), channel_id=2, replica_groups=mesh['dp'=16,'branch'=2] {'dp','branch'}, dimensions={0}, use_global_device_ids=true | all-gather | bytes 67584 | tf_op jit(solution)/shard_map/all_gather | solution.py:220
  159.5 0.8 copy-done.19
  161.3 0.9 multiply_reduce_fusion.3
  163.6 38.0 %all-gather.7 = f32[32,1,256]{2,1,0:T(1,128)S(1)} all-gather(f32[1,1,256]{2,1,0:T(1,128)S(1)} %bitcast.121), channel_id=5, replica_groups=mesh['dp'=16,'branch'=2] {'dp','branch'}, dimensions={0}, use_global_device_ids=true | all-gather | bytes 33792 | tf_op jit(solution)/shard_map/all_gather | solution.py:220
  201.6 36.6 %all-gather.6 = f32[32,1,256]{2,1,0:T(1,128)S(1)} all-gather(f32[1,1,256]{2,1,0:T(1,128)S(1)} %bitcast.119), channel_id=4, replica_groups=mesh['dp'=16,'branch'=2] {'dp','branch'}, dimensions={0}, use_global_device_ids=true | all-gather | bytes 33792 | tf_op jit(solution)/shard_map/all_gather | solution.py:220
  239.8 0.9 fusion.42
  240.7 37.2 %all-reduce.3 = (f32[256]{0:T(256)}, f32[256]{0:T(256)}) all-reduce(f32[256]{0:T(256)} %get-tuple-element.85, f32[256]{0:T(256)} %get-tuple-element.84), channel_id=1, replica_groups=mesh['dp'=16,'branch'=2] {'dp','branch'}, use_global_device_ids=true, to_apply=%region_15.16 | all-reduce | flops 512 | bytes 4096 | tf_op jit(solution)/shard_map/psum | solution.py:245
  278.0 1.5 broadcast_divide_fusion.4
  279.4 3.4 subtract_multiply_fusion.1
  282.8 2.3 fusion.56
  285.1 1.6 convert_reduce_fusion
  287.8 1.3 fusion.80
  289.7 42.9 %all-reduce.2 = (f32[512]{0:T(512)S(1)}, f32[512]{0:T(512)S(1)}) all-reduce(f32[512]{0:T(512)S(1)} %get-tuple-element.83, f32[512]{0:T(512)S(1)} %get-tuple-element.82), channel_id=1, replica_groups=mesh['dp'=16,'branch'=2] {'dp','branch'}, use_global_device_ids=true, to_apply=%region_19.20 | all-reduce | flops 1024 | bytes 8192 | tf_op jit(solution)/shard_map/psum | solution.py:266
  333.3 3.0 fusion.23
  336.4 1.3 fusion.60
  337.7 1.2 fusion.59
  340.4 1.6 reshape.179
  342.0 3.9 fusion.29
  346.4 1.3 multiply_reduce_fusion
  347.7 1.5 multiply_convert_fusion
  349.2 2.2 fusion.31
  351.4 0.8 convert_reduce_fusion.1
  352.6 1.0 fusion.73
  354.4 0.7 convert_element_type.182
  355.1 1.0 convolution_bitcast_fusion
  356.8 0.7 convert_element_type.176
  357.5 2.3 copy.133
  359.9 0.7 convert_element_type.179
  360.6 1.0 convolution_bitcast_fusion.1
  361.6 1.0 convolution_bitcast_fusion.2
  362.7 1.5 fusion.78
  364.1 1.0 copy.139
  365.2 5.0 fusion.74
  370.1 2.7 copy.123
  372.8 2.6 copy.122
  375.9 0.7 copy-done.18
  377.2 1.3 fusion.30
  378.6 2.6 copy.140
  381.1 38.5 %all-reduce.1 = (f32[5,256]{1,0:T(8,128)}, f32[256]{0:T(256)}, f32[256]{0:T(256)}, f32[512]{0:T(512)}) all-reduce(f32[5,256]{1,0:T(8,128)S(1)} %get-tuple-element.80, f32[256]{0:T(256)S(1)} %get-tuple-element.118, f32[256]{0:T(256)S(1)} %reduce_sum.230, f32[512]{0:T(512)S(1)} %copy-done.62), channel_id=1, replica_groups=mesh['dp'=16,'branch'=2] {'dp','branch'}, use_global_device_ids=true, to_apply=%region_23.24 | all-reduce | flops 2304 | bytes 18432 | tf_op jit(solution)/shard_map/psum | solution.py:279
  420.8 80.2 %all-reduce.7.cloned.1.call-done = (f32[256,256]{1,0:T(8,128)}, f32[256,256]{1,0:T(8,128)}, f32[256,256]{0,1:T(8,128)}, f32[256,256]{0,1:T(8,128)}, f32[256,256]...) async-done(((f32[256,256]{1,0:T(8,128)}, f32[256,256]{1,0:T(8,128)}, f32[256,256]{0,1:T(8,128)}, f32[256,256]{0,1:T(8,128)}, ...) | async-done | bytes 2621456 | tf_op jit(solution)/shard_map/psum | solution.py:279
  501.0 1.9 copy.141
  502.9 1.8 copy.142
  504.7 1.9 copy.143
  506.6 1.7 copy.196
  508.2 0.7 copy.197
  508.9 0.7 copy.198
  509.6 0.8 copy.199
  510.4 0.8 copy.200
  (206 shorter events, 22.5 us)
Async XLA Ops:
  7.2 45.2 %copy-start = (s32[32,64,64]{2,1,0:T(8,128)S(1)}, s32[32,64,64]{2,1,0:T(8,128)}, u32[]{:S(2)}) copy-start(s32[32,64,64]{2,1,0:T(8,128)} %param.25) | copy-start | bytes 1572868
  7.2 46.2 %copy-start.2 = (bf16[1024,256]{1,0:T(8,128)(2,1)S(1)}, bf16[1024,256]{1,0:T(8,128)(2,1)}, u32[]{:S(2)}) copy-start(bf16[1024,256]{1,0:T(8,128)(2,1)} %param.22) | copy-start | bytes 1572868
  7.2 46.4 %copy-start.41 = (bf16[1024,256]{1,0:T(8,128)(2,1)S(1)}, bf16[1024,256]{1,0:T(8,128)(2,1)}, u32[]{:S(2)}) copy-start(bf16[1024,256]{1,0:T(8,128)(2,1)} %param.23) | copy-start | bytes 1572868
  7.2 493.8 %all-reduce.7.cloned.1.call-start = ((), (), s32[]{:S(2)}) async-start(), calls=%async_computation | async-start | bytes 5242880 | tf_op jit(solution)/shard_map/psum | solution.py:279
  9.7 50.8 %copy-start.77 = (s32[5]{0:T(128)}, s32[5]{0:T(128)S(1)}, u32[]{:S(2)}) copy-start(s32[5]{0:T(128)S(1)} %iota_add_fusion) | copy-start | bytes 64
  51.7 106.4 %copy-start.56 = (f32[32]{0:T(128)}, f32[32]{0:T(128)S(1)}, u32[]{:S(2)}) copy-start(f32[32]{0:T(128)S(1)} %all-reduce) | copy-start | bytes 388
  52.3 2.3 copy-start.48
  52.3 2.3 copy-start.68
  54.7 2.2 copy-start.46
  58.1 8.1 %copy-start.8 = (bf16[16,64,8,32]{1,0,3,2:T(8,128)(2,1)}, bf16[16,64,8,32]{1,0,3,2:T(8,128)(2,1)S(1)}, u32[]{:S(2)}) copy-start(bf16[16,64,8,32]{1,0,3,2:T(8,128)(2,1)S(1)} %reshape.177) | copy-start | bytes 1572868
  58.4 2.1 copy-start.73
  60.5 4.2 copy-start.32
  66.2 9.8 %copy-start.5 = (f32[1024,256]{0,1:T(8,128)}, f32[1024,256]{0,1:T(8,128)S(1)}, u32[]{:S(2)}) copy-start(f32[1024,256]{0,1:T(8,128)S(1)} %copy.111) | copy-start | bytes 3145732
  68.7 3.1 copy-start.34
  71.8 1.9 copy-start.23
  71.8 2.0 copy-start.52
  73.8 2.2 copy-start.38
  73.8 2.2 copy-start.63
  76.9 1.4 copy-start.12
  76.9 1.4 copy-start.44
  78.7 80.1 %copy-start.64 = (f32[256]{0:T(256)S(1)}, f32[256]{0:T(256)}, u32[]{:S(2)}) copy-start(f32[256]{0:T(256)} %param.37) | copy-start | bytes 3076
  78.7 80.1 %copy-start.65 = (f32[256]{0:T(256)S(1)}, f32[256]{0:T(256)}, u32[]{:S(2)}) copy-start(f32[256]{0:T(256)} %param.30) | copy-start | bytes 3076
  78.7 80.1 %copy-start.66 = (f32[256]{0:T(256)S(1)}, f32[256]{0:T(256)}, u32[]{:S(2)}) copy-start(f32[256]{0:T(256)} %param.38) | copy-start | bytes 3076
  78.7 80.1 %copy-start.67 = (f32[256]{0:T(256)S(1)}, f32[256]{0:T(256)}, u32[]{:S(2)}) copy-start(f32[256]{0:T(256)} %param.31) | copy-start | bytes 3076
  161.3 77.0 %copy-start.57 = (f32[32]{0:T(128)S(1)}, f32[32]{0:T(128)}, u32[]{:S(2)}) copy-start(f32[32]{0:T(128)} %copy-done.56) | copy-start | bytes 388
  161.3 78.5 %copy-start.14 = (bf16[1024,256]{0,1:T(8,128)(2,1)S(1)}, bf16[1024,256]{0,1:T(8,128)(2,1)}, u32[]{:S(2)}) copy-start(bf16[1024,256]{0,1:T(8,128)(2,1)} %copy.121) | copy-start | bytes 1572868
  162.6 77.1 %copy-start.7 = (f32[1024,256]{0,1:T(8,128)}, f32[1024,256]{0,1:T(8,128)S(1)}, u32[]{:S(2)}) copy-start(f32[1024,256]{0,1:T(8,128)S(1)} %get-tuple-element.113) | copy-start | bytes 3145732
  239.0 1.7 copy-start.54
  278.0 4.9 copy-start.26
  282.8 2.3 copy-start.70
  282.8 2.3 copy-start.76
  332.6 3.7 copy-start.58
  332.6 3.7 copy-start.60
  333.3 3.1 copy-start.13
  333.3 4.4 copy-start.31
  336.4 3.1 copy-start.3
  339.8 12.4 %copy-start.27 = (bf16[1024,256]{1,0:T(8,128)(2,1)}, bf16[1024,256]{1,0:T(8,128)(2,1)S(1)}, u32[]{:S(2)}) copy-start(bf16[1024,256]{1,0:T(8,128)(2,1)S(1)} %get-tuple-element.119) | copy-start | bytes 1572868
  339.8 2.2 copy-start.53
  342.0 3.9 copy-start.24
  342.0 4.0 copy-start.35
  342.0 4.4 copy-start.36
  347.7 1.5 copy-start.11
  349.2 2.2 copy-start.9
  357.5 4.1 copy-start.15
  360.6 2.1 copy-start.17
  362.6 1.5 copy-start.29
  362.6 2.5 copy-start.33
  362.7 2.5 copy-start.74
  362.7 2.5 copy-start.78
  370.1 5.4 %copy-start.4 = (f32[1024,512]{0,1:T(8,128)S(1)}, f32[1024,512]{0,1:T(8,128)}, u32[]{:S(2)}) copy-start(f32[1024,512]{0,1:T(8,128)} %copy-done.3) | copy-start | bytes 6291460
  370.1 5.4 %copy-start.16 = (bf16[1024,256]{0,1:T(8,128)(2,1)S(1)}, bf16[1024,256]{0,1:T(8,128)(2,1)}, u32[]{:S(2)}) copy-start(bf16[1024,256]{0,1:T(8,128)(2,1)} %copy-done.15) | copy-start | bytes 1572868
  370.1 5.4 %copy-start.49 = (bf16[256,256]{1,0:T(8,128)(2,1)S(1)}, bf16[256,256]{1,0:T(8,128)(2,1)}, u32[]{:S(2)}) copy-start(bf16[256,256]{1,0:T(8,128)(2,1)} %param.32) | copy-start | bytes 393220
  372.8 3.0 copy-start.47
  375.5 1.4 copy-start.21
  375.5 1.7 copy-start.22
  375.5 1.7 copy-start.40
  378.6 2.6 copy-start.62
  378.6 41.1 %copy-start.59 = (f32[512]{0:T(512)S(1)}, f32[512]{0:T(512)}, u32[]{:S(2)}) copy-start(f32[512]{0:T(512)} %copy-done.58) | copy-start | bytes 6148
  378.6 41.7 %copy-start.61 = (f32[512]{0:T(512)S(1)}, f32[512]{0:T(512)}, u32[]{:S(2)}) copy-start(f32[512]{0:T(512)} %copy-done.60) | copy-start | bytes 6148
  501.0 7.2 %copy-start.51 = (f32[256,256]{1,0:T(8,128)S(1)}, f32[256,256]{1,0:T(8,128)}, u32[]{:S(2)}) copy-start(f32[256,256]{1,0:T(8,128)} %get-tuple-element.131) | copy-start | bytes 786436
  501.0 7.9 %copy-start.50 = (f32[256,256]{1,0:T(8,128)S(1)}, f32[256,256]{1,0:T(8,128)}, u32[]{:S(2)}) copy-start(f32[256,256]{1,0:T(8,128)} %get-tuple-element.138) | copy-start | bytes 786436
  501.0 8.7 %copy-start.43 = (f32[256,512]{1,0:T(8,128)S(1)}, f32[256,512]{1,0:T(8,128)}, u32[]{:S(2)}) copy-start(f32[256,512]{1,0:T(8,128)} %get-tuple-element.141) | copy-start | bytes 1572868
  501.0 9.4 %copy-start.42 = (f32[512,256]{1,0:T(8,128)S(1)}, f32[512,256]{1,0:T(8,128)}, u32[]{:S(2)}) copy-start(f32[512,256]{1,0:T(8,128)} %get-tuple-element.143) | copy-start | bytes 1572868
  504.7 6.6 %copy-start.1 = (s32[32,64,64]{2,1,0:T(8,128)S(1)}, s32[32,64,64]{2,1,0:T(8,128)}, u32[]{:S(2)}) copy-start(s32[32,64,64]{2,1,0:T(8,128)} %param.25) | copy-start | bytes 1572868
  (16 other events, 16.7 us)
Sparse Core Ops, SparseCore 0:
  362.7 138.1 all-reduce.6

commit v2 on v1

v2 whole, which is shorter than its diff:
```python
import functools
import math

import jax
import jax.numpy as jnp
from jax import lax
from jax.experimental import pallas as pl
from jax.experimental.pallas import tpu as pltpu
from jax.sharding import PartitionSpec as P

HEADS = 8
SLOT = 64
HALF = 128
PAIR = 2 * SLOT
GROUP = 4 * SLOT
EPSILON = 1e-05
MASKED = -1e30
MESH = pl.DeviceIdType.MESH
F32 = jnp.float32
BF16 = jnp.bfloat16


def dot(left, right):
    return jnp.dot(left, right, preferred_element_type=F32)


def dot_nt(left, right):
    return lax.dot_general(left, right, (((1,), (1,)), ((), ())), preferred_element_type=F32)


def dot_tn(left, right):
    return lax.dot_general(left, right, (((0,), (0,)), ((), ())), preferred_element_type=F32)


def sigmoid(values):
    return 0.5 * jnp.tanh(0.5 * values) + 0.5


def silu_and_slope(values):
    sigma = sigmoid(values)
    act = values * sigma
    return act, sigma + act * (1.0 - sigma)


def column_sum(values):
    return jnp.sum(values, axis=0, keepdims=True)


def twice(values):
    return jnp.concatenate([values, values], axis=1)


def put_rows(ref, index, first, vectors):
    row = first
    for vector in vectors:
        for at in range(0, vector.shape[1], HALF):
            ref[index, row : row + 1, :] = vector[:, at : at + HALF]
            row += 1


def kernel(
    dp,
    states,
    cotangent,
    counts,
    bonds,
    table,
    w1,
    b1,
    w2,
    gine_gain,
    gine_shift,
    wq,
    bq,
    wk,
    wv,
    wo,
    attn_gain,
    attn_shift,
    wup,
    bup,
    wdn,
    final_gain,
    final_shift,
    o_layer,
    o_nodes,
    o_table,
    o_w1,
    o_b1,
    o_w2,
    o_gine_gain,
    o_gine_shift,
    o_wq,
    o_bq,
    o_wk,
    o_wv,
    o_wo,
    o_attn_gain,
    o_attn_shift,
    o_wup,
    o_bup,
    o_wdn,
    o_final_gain,
    o_final_shift,
    present,
    pad,
    hot,
    slopes,
    joined,
    act,
    slope_one,
    gine_pre,
    q_s,
    k_s,
    v_s,
    probs,
    mixed,
    attn_pre,
    hidden,
    up_act,
    up_slope,
    y_s,
    down_in,
    up_in,
    jg_s,
    two_in,
    out_in,
    one_in,
    dq_s,
    dk_s,
    dv_s,
    stat_a,
    stat_b,
    stat_c,
    stat_d,
    part,
    core_in,
    half_sum,
    rs_in,
    hi_in,
    gathered,
    sem_stat_s,
    sem_stat_r,
    sem_s,
    sem_r,
):
    rows, width = states.shape
    kinds = table.shape[0]
    groups = rows // GROUP
    mols = rows // SLOT
    devices = 2 * dp
    ring = min(dp, 16)
    outer = dp // ring
    share = width // ring
    my_dp = lax.axis_index("dp")
    core = lax.axis_index("branch")
    flat = 2 * my_dp + core
    low = my_dp % ring
    high = my_dp // ring

    def device_of(place):
        return (place // 2, place % 2)

    barrier = pltpu.get_barrier_semaphore()

    def greet(k, carry):
        pl.semaphore_signal(
            barrier, inc=1, device_id=device_of((flat + k) % devices), device_id_type=MESH
        )
        return carry

    lax.fori_loop(1, devices, greet, 0)

    def round_start(ref, which, height):
        def one(k, carry):
            pltpu.make_async_remote_copy(
                src_ref=ref.at[flat, pl.ds(0, height)],
                dst_ref=ref.at[flat, pl.ds(0, height)],
                send_sem=sem_stat_s.at[which],
                recv_sem=sem_stat_r.at[which],
                device_id=device_of((flat + k) % devices),
                device_id_type=MESH,
            ).start()
            return carry

        lax.fori_loop(1, devices, one, 0)

    def round_wait(ref, which, height):
        view = ref.at[pl.ds(0, devices - 1), pl.ds(0, height)]
        pltpu.make_async_copy(view, view, sem_stat_s.at[which]).wait()
        pltpu.make_async_copy(view, view, sem_stat_r.at[which]).wait()

    def sets(which):
        return ((0, 4), (4, 3), (7, 3))[which]

    def remote(src, dst, slot, target):
        return pltpu.make_async_remote_copy(
            src_ref=src,
            dst_ref=dst,
            send_sem=sem_s.at[slot],
            recv_sem=sem_r.at[slot],
            device_id=target,
            device_id_type=MESH,
        )

    def core_start(which):
        first, many = sets(which)
        remote(
            part.at[1 - core, pl.ds(first, many)],
            core_in.at[pl.ds(first, many)],
            5 * which,
            (my_dp, 1 - core),
        ).start()

    def wait_both(view, slot):
        pltpu.make_async_copy(view, view, sem_s.at[slot]).wait()
        pltpu.make_async_copy(view, view, sem_r.at[slot]).wait()

    def core_finish(which):
        first, many = sets(which)
        wait_both(core_in.at[pl.ds(first, many)], 5 * which)
        for block in range(first, first + many):
            half_sum[block] = (
                part[core, block].astype(F32) + core_in[block].astype(F32)
            ).astype(BF16)

        def one(k, carry):
            target = (low + k) % ring
            remote(
                half_sum.at[pl.ds(first, many), pl.ds(target * share, share)],
                rs_in.at[low, pl.ds(first, many)],
                5 * which + 1,
                (high * ring + target, core),
            ).start()
            return carry

        lax.fori_loop(1, ring, one, 0)
        rs_in[low, first : first + many] = half_sum[
            first : first + many, pl.ds(low * share, share), :
        ]

    def ring_finish(which):
        first, many = sets(which)
        if ring > 1:
            wait_both(rs_in.at[pl.ds(0, ring - 1), pl.ds(first, many)], 5 * which + 1)
        total = jnp.sum(rs_in[:, first : first + many].astype(F32), axis=0)
        if outer > 1:
            hi_in[high, first : first + many] = total.astype(BF16)

            def across(k, carry):
                target = (high + k) % outer
                remote(
                    hi_in.at[high, pl.ds(first, many)],
                    hi_in.at[high, pl.ds(first, many)],
                    5 * which + 2,
                    (target * ring + low, core),
                ).start()
                return carry

            lax.fori_loop(1, outer, across, 0)
            wait_both(hi_in.at[pl.ds(0, outer - 1), pl.ds(first, many)], 5 * which + 2)
            total = jnp.sum(hi_in[:, first : first + many].astype(F32), axis=0)
        own = pl.ds(low * share, share)
        gathered[core, first : first + many, own, :] = total.astype(BF16)

        def one(k, carry):
            piece = gathered.at[core, pl.ds(first, many), own]
            remote(
                piece, piece, 5 * which + 3, (high * ring + (low + k) % ring, core)
            ).start()
            return carry

        lax.fori_loop(1, ring, one, 0)

    def gather_finish(which):
        first, many = sets(which)
        if ring > 1:
            wait_both(
                gathered.at[0, pl.ds(first, many), pl.ds(0, (ring - 1) * share)], 5 * which + 3
            )
        mine = gathered.at[core, pl.ds(first, many)]
        remote(mine, mine, 5 * which + 4, (my_dp, 1 - core)).start()

    def whole_finish(which):
        first, many = sets(which)
        wait_both(gathered.at[0, pl.ds(first, many)], 5 * which + 4)

    def put_part(block, grad):
        part[0, block] = grad[:, :HALF].astype(BF16)
        part[1, block] = grad[:, HALF:].astype(BF16)

    def read_whole(block):
        return jnp.concatenate([gathered[0, block], gathered[1, block]], axis=1).astype(F32)

    pad[...] = jnp.zeros_like(pad)
    own_total = jnp.zeros((), F32)
    for m in range(mols):
        count = counts[core * mols + m]
        own_total = own_total + count.astype(F32)
        slot = lax.broadcasted_iota(jnp.int32, (SLOT, HALF), 0)
        present[m * SLOT : (m + 1) * SLOT, :] = jnp.where(slot < count, 1.0, 0.0)
    own_inverse = 1.0 / jnp.full((1, width), own_total, F32)
    top = lax.broadcasted_iota(jnp.int32, (PAIR, HALF), 0) < SLOT
    left = lax.broadcasted_iota(jnp.int32, (1, HALF), 1) < SLOT
    lane = lax.broadcasted_iota(jnp.int32, (SLOT, HALF), 1)
    key_slot = lax.broadcasted_iota(jnp.int32, (SLOT, HALF), 0)
    head_size = width // HEADS
    per_half = HALF // head_size
    scaling = 1.0 / math.sqrt(head_size)
    to_two = scaling * math.log2(math.e)
    zero16 = jnp.zeros((PAIR, HALF), BF16)

    def spread(value):
        return jnp.concatenate(
            [jnp.where(top, value, zero16), jnp.where(top, zero16, value)], axis=1
        )

    def by_head(value):
        blocks = []
        for h in range(per_half):
            inside = (lane >= h * head_size) & (lane < (h + 1) * head_size)
            blocks.append(
                jnp.concatenate(
                    [
                        jnp.where(inside, value[:SLOT], zero16[:SLOT]),
                        jnp.where(inside, value[SLOT:], zero16[:SLOT]),
                    ],
                    axis=1,
                )
            )
        return jnp.concatenate(blocks, axis=0)

    def pick_rows(value):
        return jnp.where(top, value[:, :HALF], value[:, HALF:])

    def pick_heads(value):
        parts = []
        for side in range(2):
            total = jnp.zeros((SLOT, HALF), F32)
            for h in range(per_half):
                inside = (lane >= h * head_size) & (lane < (h + 1) * head_size)
                block = value[h * SLOT : (h + 1) * SLOT, side * HALF : (side + 1) * HALF]
                total = jnp.where(inside, block, total)
            parts.append(total)
        return jnp.concatenate(parts, axis=0)

    def forward(g, sums):
        at = pl.ds(pl.multiple_of(g * GROUP, GROUP), GROUP)
        x = states[at, :]
        xf = x.astype(F32)
        q_s[at, :] = (dot(x, wq[...]) + bq[...]).astype(BF16)
        k_s[at, :] = dot(x, wk[...]).astype(BF16)
        v_s[at, :] = dot(x, wv[...]).astype(BF16)
        for p in range(2):
            pair = 2 * g + p
            rows_at = pl.ds(pl.multiple_of(g * GROUP + p * PAIR, PAIR), PAIR)
            mol = core * mols + 2 * pair
            pad[0:SLOT, 0:SLOT] = bonds[mol]
            pad[SLOT:PAIR, SLOT:PAIR] = bonds[mol + 1]
            kind = pad[...]
            xp = xf[p * PAIR : (p + 1) * PAIR]
            hots, sents = [], []
            for t in range(kinds):
                one = jnp.where(kind == t + 1, 1.0, 0.0).astype(BF16)
                hot[pair, t] = one
                sent, slope = silu_and_slope(xp + table[t : t + 1, :])
                slopes[pair, t] = slope.astype(BF16)
                hots.append(one)
                sents.append(sent.astype(BF16))
            message = dot(jnp.concatenate(hots, axis=1), jnp.concatenate(sents, axis=0))
            joined[rows_at, :] = (xp + message).astype(BF16)
        first, slope = silu_and_slope(dot(joined[at, :], w1[...]) + b1[...])
        slope_one[at, :] = slope.astype(BF16)
        first = first.astype(BF16)
        act[at, :] = first
        live = twice(present[at, :])
        pre = dot(first, w2[...]) + xf
        gine_pre[at, :] = pre
        sum_gine = sums[0] + column_sum(live * pre)
        for p in range(2):
            pair = 2 * g + p
            rows_at = pl.ds(pl.multiple_of(g * GROUP + p * PAIR, PAIR), PAIR)
            mol = core * mols + 2 * pair
            alive = key_slot < jnp.where(left, counts[mol], counts[mol + 1])
            for side in range(2):
                cols = slice(side * HALF, (side + 1) * HALF)
                scores = dot_nt(by_head(k_s[rows_at, cols]), spread(q_s[rows_at, cols]))
                scores = scores.reshape(per_half, SLOT, HALF)
                scores = jnp.where(alive[None], scores, MASKED)
                peak = jnp.max(scores, axis=1, keepdims=True)
                powers = jnp.exp2((scores - peak) * to_two)
                weights = powers * (1.0 / jnp.sum(powers, axis=1, keepdims=True))
                weights = weights.reshape(per_half * SLOT, HALF).astype(BF16)
                probs[pair, side] = weights
                mixed[rows_at, cols] = pick_rows(
                    dot_tn(weights, by_head(v_s[rows_at, cols]))
                ).astype(BF16)
        pre = dot(mixed[at, :], wo[...]) + xf
        attn_pre[at, :] = pre
        return (sum_gine, sums[1] + column_sum(live * pre))

    nothing = jnp.zeros((1, width), F32)
    sum_gine, sum_attn = lax.fori_loop(0, groups, forward, (nothing, nothing))
    mean_gine, mean_attn = sum_gine * own_inverse, sum_attn * own_inverse

    def squares(g, sums):
        at = pl.ds(pl.multiple_of(g * GROUP, GROUP), GROUP)
        live = twice(present[at, :])
        one, two = live * (gine_pre[at, :] - mean_gine), live * (attn_pre[at, :] - mean_attn)
        return (sums[0] + column_sum(one * one), sums[1] + column_sum(two * two))

    square_gine, square_attn = lax.fori_loop(0, groups, squares, (nothing, nothing))
    put_rows(stat_a, flat, 0, (mean_gine, mean_attn, square_gine, square_attn))
    stat_a[flat, 8:9, :] = jnp.full((1, HALF), own_total, F32)
    pl.semaphore_wait(barrier, devices - 1)
    round_start(stat_a, 0, 9)

    def merged(ref, many):
        count = stat_a[:, 8:9, :]
        node_total = jnp.sum(count, axis=0)
        means = ref[:, 0:many, :]
        mean = jnp.sum(means * count, axis=0) / node_total
        offset = means - mean[None]
        square = jnp.sum(ref[:, many : 2 * many, :] + count * offset * offset, axis=0)
        return mean, lax.rsqrt(square / node_total + EPSILON), node_total

    def vector(value, row):
        return jnp.concatenate([value[row : row + 1], value[row + 1 : row + 2]], axis=1)

    round_wait(stat_a, 0, 9)
    mean, rstd, node_total = merged(stat_a, 4)
    inverse = twice(1.0 / node_total)
    mean_gine, mean_attn = vector(mean, 0), vector(mean, 2)
    rstd_gine, rstd_attn = vector(rstd, 0), vector(rstd, 2)
    scale_gine = gine_gain[...] * rstd_gine
    scale_attn = attn_gain[...] * rstd_attn

    def feed(g, sums):
        at = pl.ds(pl.multiple_of(g * GROUP, GROUP), GROUP)
        live = twice(present[at, :])
        h = live * (
            scale_gine * (gine_pre[at, :] - mean_gine)
            + gine_shift[...]
            + scale_attn * (attn_pre[at, :] - mean_attn)
            + attn_shift[...]
        )
        h16 = h.astype(BF16)
        hidden[at, :] = h16
        value, slope = silu_and_slope(dot(h16, wup[...]) + bup[...])
        value = value.astype(BF16)
        up_act[at, :] = value
        up_slope[at, :] = slope.astype(BF16)
        y = h + dot(value, wdn[...])
        y_s[at, :] = y
        return (
            sums[0] + column_sum(live * y),
            sums[1] + column_sum(live * cotangent[at, :].astype(F32)),
        )

    sum_y, sum_c = lax.fori_loop(0, groups, feed, (nothing, nothing))
    mean_y = sum_y * own_inverse

    def spread_y(g, sums):
        at = pl.ds(pl.multiple_of(g * GROUP, GROUP), GROUP)
        live = twice(present[at, :])
        offset = live * (y_s[at, :] - mean_y)
        return (
            sums[0] + column_sum(offset * offset),
            sums[1] + column_sum(offset * cotangent[at, :].astype(F32)),
        )

    square_y, cross_y = lax.fori_loop(0, groups, spread_y, (nothing, nothing))
    put_rows(stat_b, flat, 0, (mean_y, square_y, sum_c, cross_y))
    round_start(stat_b, 1, 8)
    round_wait(stat_b, 1, 8)
    mean, rstd, _ = merged(stat_b, 2)
    moved = stat_b[:, 0:2, :] - mean[None]
    c_total = jnp.sum(stat_b[:, 4:6, :], axis=0)
    c_gain = jnp.sum(stat_b[:, 6:8, :] + moved * stat_b[:, 4:6, :], axis=0) * rstd
    mean_y, rstd_y = vector(mean, 0), vector(rstd, 0)
    c_shift, c_gain = vector(c_total, 0), vector(c_gain, 0)
    o_final_shift[...] = c_shift
    o_final_gain[...] = c_gain

    scale_y = final_gain[...] * rstd_y
    shift_part, gain_part = c_shift * inverse, c_gain * inverse

    def feed_back(g, sums):
        at = pl.ds(pl.multiple_of(g * GROUP, GROUP), GROUP)
        live = twice(present[at, :])
        hat = (y_s[at, :] - mean_y) * rstd_y
        o_layer[at, :] = (live * (final_gain[...] * hat + final_shift[...])).astype(BF16)
        grad = (live * scale_y) * (cotangent[at, :].astype(F32) - shift_part - hat * gain_part)
        grad16 = grad.astype(BF16)
        down_in[at, :] = grad16
        inner = (dot_nt(grad16, wdn[...]) * up_slope[at, :].astype(F32)).astype(BF16)
        up_in[at, :] = inner
        back = (grad + dot_nt(inner, wup[...])).astype(BF16)
        jg_s[at, :] = back
        back = back.astype(F32)
        return (
            sums[0] + column_sum(back),
            sums[1] + column_sum(back * (gine_pre[at, :] - mean_gine)),
            sums[2] + column_sum(back * (attn_pre[at, :] - mean_attn)),
            sums[3] + column_sum(inner.astype(F32)),
        )

    wide = jnp.zeros((1, wup.shape[1]), F32)
    sum_j, cross_gine, cross_attn, sum_up = lax.fori_loop(
        0, groups, feed_back, (nothing, nothing, nothing, wide)
    )
    put_rows(stat_c, flat, 0, (sum_j, cross_gine * rstd_gine, cross_attn * rstd_attn, sum_up))
    round_start(stat_c, 2, 10)

    up_grad = dot_tn(hidden[...], up_in[...])
    put_part(0, up_grad[:, :width])
    put_part(1, up_grad[:, width:])
    for at in range(2):
        put_part(2 + at, dot_tn(up_act[:, at * width : (at + 1) * width], down_in[...]))
    core_start(0)

    round_wait(stat_c, 2, 10)
    sums = jnp.sum(stat_c[:, 0:10, :], axis=0)
    shift_sum, gain_gine, gain_attn = vector(sums, 0), vector(sums, 2), vector(sums, 4)
    o_gine_shift[...] = shift_sum
    o_attn_shift[...] = shift_sum
    o_gine_gain[...] = gain_gine
    o_attn_gain[...] = gain_attn
    o_bup[...] = jnp.concatenate([vector(sums, 6), vector(sums, 8)], axis=1)
    core_finish(0)

    shift_part = shift_sum * inverse
    gine_part, attn_part = gain_gine * inverse * rstd_gine, gain_attn * inverse * rstd_attn

    def back_one(g, sums):
        at = pl.ds(pl.multiple_of(g * GROUP, GROUP), GROUP)
        live = twice(present[at, :])
        base = jg_s[at, :].astype(F32) - shift_part
        one = (live * scale_gine) * (base - (gine_pre[at, :] - mean_gine) * gine_part)
        two = (live * scale_attn) * (base - (attn_pre[at, :] - mean_attn) * attn_part)
        o_nodes[at, :] = one + two
        one = one.astype(BF16)
        two_in[at, :] = one
        out_in[at, :] = two.astype(BF16)
        inner = (dot_nt(one, w2[...]) * slope_one[at, :].astype(F32)).astype(BF16)
        one_in[at, :] = inner
        return sums + column_sum(inner.astype(F32))

    sum_one = lax.fori_loop(0, groups, back_one, nothing)
    put_part(4, dot_tn(act[...], two_in[...]))
    put_part(5, dot_tn(mixed[...], out_in[...]))
    put_part(6, dot_tn(joined[...], one_in[...]))
    core_start(1)
    ring_finish(0)

    def back_attend(g, sums):
        at = pl.ds(pl.multiple_of(g * GROUP, GROUP), GROUP)
        mixed_grad = dot_nt(out_in[at, :], wo[...]).astype(BF16)
        for p in range(2):
            pair = 2 * g + p
            rows_at = pl.ds(pl.multiple_of(g * GROUP + p * PAIR, PAIR), PAIR)
            for side in range(2):
                cols = slice(side * HALF, (side + 1) * HALF)
                grad = spread(mixed_grad[p * PAIR : (p + 1) * PAIR, cols])
                weights = probs[pair, side]
                probs_grad = dot_nt(by_head(v_s[rows_at, cols]), grad)
                dv_s[rows_at, cols] = pick_heads(dot(weights, grad)).astype(BF16)
                soft = weights.astype(F32).reshape(per_half, SLOT, HALF)
                probs_grad = probs_grad.reshape(per_half, SLOT, HALF)
                inner = jnp.sum(soft * probs_grad, axis=1, keepdims=True)
                score_grad = (soft * (probs_grad - inner)).astype(BF16)
                score_grad = score_grad.reshape(per_half * SLOT, HALF)
                dk_s[rows_at, cols] = (
                    pick_heads(dot(score_grad, spread(q_s[rows_at, cols]))) * scaling
                ).astype(BF16)
                dq_s[rows_at, cols] = (
                    pick_rows(dot_tn(score_grad, by_head(k_s[rows_at, cols]))) * scaling
                ).astype(BF16)
        return sums + column_sum(dq_s[at, :].astype(F32))

    sum_q = lax.fori_loop(0, groups, back_attend, nothing)
    put_part(7, dot_tn(states[...], dq_s[...]))
    put_part(8, dot_tn(states[...], dk_s[...]))
    put_part(9, dot_tn(states[...], dv_s[...]))
    core_start(2)
    core_finish(1)
    gather_finish(0)

    def back_nodes(g, sums):
        at = pl.ds(pl.multiple_of(g * GROUP, GROUP), GROUP)
        joined_back = dot_nt(one_in[at, :], w1[...])
        message_grad = joined_back.astype(BF16)
        pieces = []
        for p in range(2):
            pair = 2 * g + p
            sent_grad = dot(
                hot[pair].reshape(kinds * PAIR, PAIR), message_grad[p * PAIR : (p + 1) * PAIR]
            )
            piece = joined_back[p * PAIR : (p + 1) * PAIR]
            for t in range(kinds):
                shifted = sent_grad[t * PAIR : (t + 1) * PAIR] * slopes[pair, t].astype(F32)
                piece = piece + shifted
                sums = sums[:t] + (sums[t] + column_sum(shifted),) + sums[t + 1 :]
            pieces.append(piece)
        o_nodes[at, :] += (
            jnp.concatenate(pieces, axis=0)
            + dot_nt(dq_s[at, :], wq[...])
            + dot_nt(dk_s[at, :], wk[...])
            + dot_nt(dv_s[at, :], wv[...])
        )
        return sums

    table_sums = lax.fori_loop(0, groups, back_nodes, (nothing,) * kinds)
    put_rows(stat_d, flat, 0, (sum_one, sum_q) + table_sums)
    height = 4 + 2 * kinds
    round_start(stat_d, 3, height)

    core_finish(2)
    ring_finish(1)
    ring_finish(2)
    whole_finish(0)
    o_wup[...] = jnp.concatenate([read_whole(0), read_whole(1)], axis=1)
    o_wdn[...] = jnp.concatenate([read_whole(2), read_whole(3)], axis=0)
    gather_finish(1)
    gather_finish(2)
    round_wait(stat_d, 3, height)
    sums = jnp.sum(stat_d[:, 0:height, :], axis=0)
    o_b1[...] = vector(sums, 0)
    o_bq[...] = vector(sums, 2)
    for t in range(kinds):
        o_table[t : t + 1, :] = vector(sums, 4 + 2 * t)
    whole_finish(1)
    o_w2[...] = read_whole(4)
    o_wo[...] = read_whole(5)
    o_w1[...] = read_whole(6)
    whole_finish(2)
    o_wq[...] = read_whole(7)
    o_wk[...] = read_whole(8)
    o_wv[...] = read_whole(9)


def layer(dp, *arrays):
    states, cotangent, counts, bonds, table, *rest = arrays
    rows, width = states.shape
    kinds = table.shape[0]
    inner = arrays[17].shape[1]
    pairs = rows // PAIR
    devices = 2 * dp
    ring = min(dp, 16)
    share = width // ring
    blocks = 10
    flat = [item.reshape(1, -1) if item.ndim == 1 else item for item in rest]

    def row(size):
        return jax.ShapeDtypeStruct((1, size), F32)

    def square(*shape):
        return jax.ShapeDtypeStruct(shape, F32)

    big = square(width, width)
    out_shape = (
        jax.ShapeDtypeStruct((rows, width), BF16),
        square(rows, width),
        square(kinds, width),
        big,
        row(width),
        big,
        row(width),
        row(width),
        big,
        row(width),
        big,
        big,
        big,
        row(width),
        row(width),
        square(width, inner),
        row(inner),
        square(inner, width),
        row(width),
        row(width),
    )

    def half_rows(columns=width):
        return pltpu.VMEM((rows, columns), BF16)

    def full_rows(columns=width):
        return pltpu.VMEM((rows, columns), F32)

    scratch = [
        full_rows(HALF),
        pltpu.VMEM((PAIR, PAIR), jnp.int32),
        pltpu.VMEM((pairs, kinds, PAIR, PAIR), BF16),
        pltpu.VMEM((pairs, kinds, PAIR, width), BF16),
        half_rows(),
        half_rows(),
        half_rows(),
        full_rows(),
        half_rows(),
        half_rows(),
        half_rows(),
        pltpu.VMEM((pairs, 2, 4 * SLOT, HALF), BF16),
        half_rows(),
        full_rows(),
        half_rows(),
        half_rows(inner),
        half_rows(inner),
        full_rows(),
        half_rows(),
        half_rows(inner),
        half_rows(),
        half_rows(),
        half_rows(),
        half_rows(),
        half_rows(),
        half_rows(),
        half_rows(),
        pltpu.VMEM((devices, 16, HALF), F32),
        pltpu.VMEM((devices, 8, HALF), F32),
        pltpu.VMEM((devices, 16, HALF), F32),
        pltpu.VMEM((devices, 16, HALF), F32),
        pltpu.VMEM((2, blocks, width, HALF), BF16),
        pltpu.VMEM((blocks, width, HALF), BF16),
        pltpu.VMEM((blocks, width, HALF), BF16),
        pltpu.VMEM((ring, blocks, share, HALF), BF16),
        pltpu.VMEM((dp // ring, blocks, share, HALF), BF16),
        pltpu.VMEM((2, blocks, width, HALF), BF16),
        pltpu.SemaphoreType.DMA((4,)),
        pltpu.SemaphoreType.DMA((4,)),
        pltpu.SemaphoreType.DMA((15,)),
        pltpu.SemaphoreType.DMA((15,)),
    ]
    vmem = pl.BlockSpec(memory_space=pltpu.VMEM)
    in_specs = [vmem] * len(arrays)
    in_specs[2] = pl.BlockSpec(memory_space=pltpu.SMEM)
    outs = pl.pallas_call(
        functools.partial(kernel, dp),
        out_shape=out_shape,
        in_specs=in_specs,
        out_specs=(vmem,) * len(out_shape),
        scratch_shapes=scratch,
        compiler_params=pltpu.CompilerParams(
            collective_id=0, has_side_effects=True, vmem_limit_bytes=60 * 1024 * 1024
        ),
        name="layer",
    )(states, cotangent, counts, bonds, table, *flat)
    flat_places = (4, 6, 7, 9, 13, 14, 16, 18, 19)
    return tuple(item[0] if i in flat_places else item for i, item in enumerate(outs))


def solution(mesh):
    rows, whole = P(("dp", "branch"), None), P()
    placed = (rows, rows, P("dp"), P("dp", None, None)) + (whole,) * 18
    return jax.shard_map(
        functools.partial(layer, mesh.shape["dp"]),
        mesh=mesh,
        in_specs=placed,
        out_specs=(rows, rows) + (whole,) * 18,
        check_vma=False,
    )
```

time: 528 us -> 94.6 us (0.18); the launches traced: 519 us -> 94.3 us
  blocking collectives: 313 us -> 0 us
  waiting for transfers between devices: 80.2 us -> 0 us
  Pallas kernels: 0 us -> 78.5 us
  matrix products: 40.5 us -> 0 us
  local copies, waits for them, and re-layouts: 48 us -> 15.1 us
  other arithmetic: 21.8 us -> 0 us
  between operations: 15.4 us -> 0.71 us
    all_gather x4 -> x0, blocking collectives: 152 us -> none  [merge(): means, squares, totals = lax.all_gather(stats, axes, axis=0)]
    psum x3 -> x0, blocking collectives: 119 us -> none  [the longest x1 42.9 us: body(): lax.psum((jnp.sum(twice, axis=0), jnp.sum(twice * hat, axis=0)), axes)]
    psum x1 -> x0, waiting for transfers between devices: 80.2 us -> none  [body(): lax.psum((*gine_grads, *attn_grads, up_grad, up_bias_grad, down_grad), axes)]
    pallas_call x0 -> x1, Pallas kernels: none -> 78.5 us  [layer(): pl.pallas_call(functools.partial(kernel, dp), out_shape=out_shape, in_spe...]
    unnamed x1 -> x0, blocking collectives: 42 us -> none
    dot_general x32 -> x0, matrix products: 40.5 us -> none  [the longest x1 4.95 us: gine_backward(): jnp.einsum('tgij,gid->tgjd', onehot, message_grad, preferred_element_type...]
    convert_element_type x14 -> x0, local copies, waits for them, and re-layouts: 9.13 us -> none  [the longest x2 3.06 us: attend_backward(): key_grad = (jnp.einsum('ghij,gihe->gjhe', score_grad, query, preferred_el...]
    unnamed x172 -> x58, local copies, waits for them, and re-layouts: 23.3 us -> 15.1 us
  transfers between devices with their start and end apart: 1 -> 0, of which waited for: 1 -> 0; matrix products, arithmetic and copies ran while one was open for 4% -> 0% of each run, Pallas kernels for 0% -> 0%
where the time goes in v2:
time: 94.6 us; the launch traced here: 94.3 us
  Pallas kernels  78.5 us (83%)
  local copies, waits for them, and re-layouts  15.1 us (16%)
    pallas_call x1, Pallas kernels, layer(): pl.pallas_call(functools.partial(kernel, dp), out_shape=out_shape, in_spe...  78.5 us
    unnamed x58, local copies, waits for them, and re-layouts  15.1 us

profile of v2, /device:TPU:0, one launch (start us, length us, event | category | flops | bytes accessed | tf_op | source)
XLA Modules:
  0.0 94.3 jit_solution(9117289033614684733)
XLA Ops:
  0.7 78.5 %layer.1 = (bf16[1024,256]{1,0:T(8,128)(2,1)}, f32[1024,256]{1,0:T(8,128)}, f32[5,256]{1,0:T(8,128)}, f32[256,256]{1,0:T(8,128)}, f32[1,256]{1,0:T(1,128)}, /*in...) custom-call(bf16[1024,256]{1,0:T(8,128)(2,1)} %states.1, ...), custom_call_target="tpu_custom_call" | custom-call | tf_op jit(solution)/shard_map/layer/pallas_call | solution.py:736
  79.1 0.0 copy-start
  79.2 2.0 %copy.62 = bf16[1024,256]{1,0:T(8,128)(2,1)} copy(bf16[1024,256]{1,0:T(8,128)(2,1)} %get-tuple-element.80) | data formatting | bytes 1048576
  81.1 0.0 copy-done
  81.1 0.0 copy-start.9
  81.1 0.0 copy-start.8
  81.1 1.0 %copy.63 = f32[1024,256]{1,0:T(8,128)} copy(f32[1024,256]{1,0:T(8,128)S(1)} %copy-done) | data formatting | bytes 2097152
  82.1 0.0 copy-done.9
  82.1 0.6 copy.64
  82.7 0.0 copy-done.8
  82.7 0.0 copy-start.18
  82.7 0.0 copy-start.7
  82.7 0.7 copy.65
  83.4 0.0 copy-done.18
  83.4 0.6 copy.66
  84.0 0.0 copy-done.7
  84.0 0.0 copy-start.17
  84.0 0.0 copy-start.6
  84.0 0.7 copy.67
  84.7 0.0 copy-done.17
  84.7 0.0 copy-start.16
  84.7 0.6 copy.68
  85.2 0.1 copy-done.16
  85.4 0.6 copy.69
  85.9 0.0 copy-done.6
  85.9 0.0 copy-start.15
  85.9 0.0 copy-start.5
  85.9 0.7 copy.70
  86.6 0.0 copy-done.15
  86.6 0.6 copy.71
  87.2 0.0 copy-done.5
  87.2 0.0 copy-start.4
  87.2 0.0 copy-start.3
  87.2 0.7 copy.72
  87.9 0.3 copy-done.4
  88.2 0.0 copy-start.2
  88.3 0.7 copy.73
  89.0 0.0 copy-done.3
  89.0 0.0 copy-start.14
  89.0 0.7 copy.74
  89.7 0.0 copy-done.14
  89.7 0.0 copy-start.13
  89.7 0.6 copy.75
  90.2 0.1 copy-done.13
  90.3 0.6 copy.76
  90.9 0.0 copy-done.2
  90.9 0.0 copy-start.10
  90.9 0.0 copy-start.1
  90.9 0.8 copy.77
  91.7 0.0 copy-done.10
  91.7 0.6 copy.78
  92.3 0.0 copy-done.1
  92.3 0.0 copy-start.12
  92.3 0.8 copy.79
  93.1 0.0 copy-done.12
  93.1 0.0 copy-start.11
  93.1 0.6 copy.80
  93.6 0.1 copy-done.11
  93.7 0.6 copy.81
Async XLA Ops:
  79.1 2.0 %copy-start = (f32[1024,256]{1,0:T(8,128)S(1)}, f32[1024,256]{1,0:T(8,128)}, u32[]{:S(2)}) copy-start(f32[1024,256]{1,0:T(8,128)} %get-tuple-element.81) | copy-start | bytes 3145732
  81.1 1.0 %copy-start.9 = (f32[5,256]{1,0:T(8,128)S(1)}, f32[5,256]{1,0:T(8,128)}, u32[]{:S(2)}) copy-start(f32[5,256]{1,0:T(8,128)} %get-tuple-element.82) | copy-start | bytes 15364
  81.1 1.6 %copy-start.8 = (f32[256,256]{1,0:T(8,128)S(1)}, f32[256,256]{1,0:T(8,128)}, u32[]{:S(2)}) copy-start(f32[256,256]{1,0:T(8,128)} %get-tuple-element.83) | copy-start | bytes 786436
  82.7 0.7 copy-start.18
  82.7 1.3 %copy-start.7 = (f32[256,256]{1,0:T(8,128)S(1)}, f32[256,256]{1,0:T(8,128)}, u32[]{:S(2)}) copy-start(f32[256,256]{1,0:T(8,128)} %get-tuple-element.85) | copy-start | bytes 786436
  84.0 0.7 copy-start.17
  84.0 2.0 %copy-start.6 = (f32[256,256]{1,0:T(8,128)S(1)}, f32[256,256]{1,0:T(8,128)}, u32[]{:S(2)}) copy-start(f32[256,256]{1,0:T(8,128)} %get-tuple-element.88) | copy-start | bytes 786436
  84.7 0.7 copy-start.16
  85.9 0.7 copy-start.15
  85.9 1.3 %copy-start.5 = (f32[256,256]{1,0:T(8,128)S(1)}, f32[256,256]{1,0:T(8,128)}, u32[]{:S(2)}) copy-start(f32[256,256]{1,0:T(8,128)} %get-tuple-element.90) | copy-start | bytes 786436
  87.2 1.0 %copy-start.4 = (f32[256,256]{1,0:T(8,128)S(1)}, f32[256,256]{1,0:T(8,128)}, u32[]{:S(2)}) copy-start(f32[256,256]{1,0:T(8,128)} %get-tuple-element.91) | copy-start | bytes 786436
  87.2 1.8 %copy-start.3 = (f32[256,256]{1,0:T(8,128)S(1)}, f32[256,256]{1,0:T(8,128)}, u32[]{:S(2)}) copy-start(f32[256,256]{1,0:T(8,128)} %get-tuple-element.92) | copy-start | bytes 786436
  88.2 2.6 %copy-start.2 = (f32[256,512]{1,0:T(8,128)S(1)}, f32[256,512]{1,0:T(8,128)}, u32[]{:S(2)}) copy-start(f32[256,512]{1,0:T(8,128)} %get-tuple-element.95) | copy-start | bytes 1572868
  89.0 0.7 copy-start.14
  89.7 0.7 copy-start.13
  90.9 0.8 copy-start.10
  90.9 1.4 %copy-start.1 = (f32[512,256]{1,0:T(8,128)S(1)}, f32[512,256]{1,0:T(8,128)}, u32[]{:S(2)}) copy-start(f32[512,256]{1,0:T(8,128)} %get-tuple-element.97) | copy-start | bytes 1572868
  92.3 0.8 copy-start.12
  93.1 0.7 copy-start.11
